TPU v7x, 32 devices: a whole 2x2x4 slice. The times are simulated.
32 devices in a mesh: sec: 4 (over y, x), dom: 8 (over z, core).
Axes of the slice: x: 2, y: 2, z: 4, core: 2. Of those that a mesh axis runs over, the one named last changes fastest.
Arguments:
- spectrum: bfloat16 [1296, 4096], P(None, ('sec', 'dom')), may hold values from 0.099609375 to 2
- surface_wind: float32 [2, 4096], P(None, ('sec', 'dom')), may hold values from -30 to 30
- wet_mask: float32 [4096], P(('sec', 'dom')), may hold values from 0.5 to 1
- block_order: int32 [32], P(('sec', 'dom')), may hold values from 0 to 7, as said below
Outputs:
- new_spectrum: bfloat16 [1296, 4096], P(None, ('sec', 'dom'))
- wave_stress: float32 [2, 4096], P(None, ('sec', 'dom'))
Inputs may be any that keep to these rules, and one draw needn't show every extreme that they name: `block_order`: each aligned block of 8 entries, those of one section, is a permutation of 0 to 7.
All inputs are finite; a program needn't handle non-finite values.
Results may differ from a plain program's by a relative error of at most 0.0041.
Values may be sent and summed in bfloat16 or wider, within the bound.
No kernel may reach another device: no remote copies, remote signals or barrier semaphores. Data moves between devices by JAX's collectives and lax.ppermute only.
A program may use at most 64 MiB of HBM per device.

v0:
```python
import math

import jax
import jax.numpy as jnp
from jax import lax
from jax.sharding import PartitionSpec as P

NF = 36
ND = 36
LAT = 128
SUBSTEPS = 4


gravity = 9.81
base_freq = 0.035
freq_growth = 1.1
wind_rate = 0.015
dissip_rate = 0.008
steep_ref = 3.0
stress_coef = 0.01
courant = 0.62


def padded(block, sides, width):
    for axis, dim in sides:
        count = lax.axis_size(axis)
        forward = [(i, i + 1) for i in range(count - 1)]
        forward.append((count - 1, 0))
        backward = [(target, source) for source, target in forward]
        low = lax.ppermute(
            lax.slice_in_dim(block, block.shape[dim] - width, None, axis=dim), axis, forward
        )
        high = lax.ppermute(lax.slice_in_dim(block, 0, width, axis=dim), axis, backward)
        block = jnp.concatenate([low, block, high], axis=dim)
    return block


def bin_tables(bin_index, freq_count, dir_count):
    total = freq_count * dir_count
    is_real = bin_index < total
    clamped = jnp.minimum(bin_index, total - 1)
    freq_pos = (clamped // dir_count).astype(jnp.float32)
    dir_pos = (clamped % dir_count).astype(jnp.float32)
    slowing = jnp.exp(-freq_pos * math.log(freq_growth))
    radian_freq = 2.0 * math.pi * base_freq / slowing
    wavenum = radian_freq * radian_freq / gravity
    phase_speed = gravity / radian_freq
    direction = dir_pos * (2.0 * math.pi / dir_count)
    dir_cos = jnp.cos(direction)
    dir_sin = jnp.sin(direction)
    bin_area = jnp.where(is_real, 0.1 * radian_freq * (2.0 * math.pi / dir_count), 0.0)
    travel = jnp.where(is_real, courant * slowing, 0.0)
    return (
        bin_area,
        radian_freq,
        wavenum,
        phase_speed,
        dir_cos,
        dir_sin,
        travel * dir_cos,
        travel * dir_sin,
    )


def source_parts(spectra, wind_east, wind_north, tables):
    bin_area, radian_freq, wavenum, phase_speed, dir_cos, dir_sin = tables[:6]
    energy = spectra.astype(jnp.float32)
    weighted = bin_area[:, None] * energy
    moments = jnp.stack(
        [
            jnp.sum(weighted, axis=0),
            jnp.sum(weighted / radian_freq[:, None], axis=0),
            jnp.sum(weighted / jnp.sqrt(wavenum)[:, None], axis=0),
        ]
    )
    along = dir_cos[:, None] * wind_east[None, :] + dir_sin[:, None] * wind_north[None, :]
    growth = radian_freq[:, None] * jnp.maximum(0.0, 1.2 * along / phase_speed[:, None] - 1.0)
    flux_in = weighted * growth / phase_speed[:, None]
    momentum = jnp.stack(
        [jnp.sum(flux_in * dir_cos[:, None], axis=0), jnp.sum(flux_in * dir_sin[:, None], axis=0)]
    )
    return (moments, growth, momentum)


def apply_sources(spectra, wetness, moments, growth, tables):
    wavenum = tables[2]
    mean_freq = moments[0] / moments[1]
    mean_wavenum = (moments[0] / moments[2]) ** 2
    steepness = moments[0] * mean_wavenum * mean_wavenum
    ratio = wavenum[:, None] / mean_wavenum[None, :]
    decay = (mean_freq * (steepness / steep_ref) ** 2)[None, :] * (
        0.5 * ratio + 0.5 * ratio * ratio
    )
    energy = spectra.astype(jnp.float32)
    return (wetness[None, :] * energy * jnp.exp(wind_rate * growth - dissip_rate * decay)).astype(
        jnp.bfloat16
    )


def advance(middle, from_west, from_east, speed_x, speed_y):
    lead = [(0, 0)] * (middle.ndim - 1)
    from_south = jnp.pad(middle[..., :-1], lead + [(1, 0)])
    from_north = jnp.pad(middle[..., 1:], lead + [(0, 1)])
    remain = 1.0 - jnp.abs(speed_x) - jnp.abs(speed_y)
    return (
        remain * middle
        + jnp.maximum(speed_x, 0.0) * from_west
        + jnp.maximum(-speed_x, 0.0) * from_east
        + jnp.maximum(speed_y, 0.0) * from_south
        + jnp.maximum(-speed_y, 0.0) * from_north
    )


def on_device(spectrum, surface_wind, wet_mask, block_order):
    bin_count = spectrum.shape[0]
    point_count = spectrum.shape[1]
    block_count = point_count // LAT
    dom_count = lax.axis_size("dom")
    dom_rank = lax.axis_index("dom")
    bins_each = (bin_count + dom_count - 1) // dom_count
    padding = bins_each * dom_count - bin_count
    order_all = lax.all_gather(block_order, "dom", axis=0, tiled=True)
    column_count = order_all.shape[0]
    inverse = (
        jnp.zeros((column_count,), jnp.int32)
        .at[order_all]
        .set(jnp.arange(column_count, dtype=jnp.int32))
    )
    wind_flat, wet_flat = (
        lax.all_gather(surface_wind, "dom", axis=1, tiled=True),
        lax.all_gather(wet_mask, "dom", axis=0, tiled=True),
    )
    wet_grid = wet_flat.reshape(column_count, LAT)
    wind_all = wind_flat.reshape(2, column_count, LAT)
    local_bins = dom_rank * bins_each + jnp.arange(bins_each, dtype=jnp.int32)
    own_tables = bin_tables(local_bins, NF, ND)
    own_columns = lax.dynamic_slice_in_dim(order_all, dom_rank * block_count, block_count, 0)
    wind_own = wind_all[:, own_columns].reshape(2, point_count)
    wet_own = wet_grid[own_columns].reshape(point_count)
    all_tables = bin_tables(jnp.arange(bin_count, dtype=jnp.int32), NF, ND)
    moments, growth, momentum = source_parts(spectrum, wind_own[0], wind_own[1], all_tables)
    renewed = apply_sources(spectrum, wet_own, moments, growth, all_tables)
    in_bins = lax.all_to_all(
        jnp.pad(renewed, ((0, padding), (0, 0))), "dom", split_axis=0, concat_axis=1, tiled=True
    )
    stress_store = lax.all_gather(stress_coef * momentum, "dom", axis=1, tiled=True).reshape(
        2, column_count, LAT
    )
    speed_x = own_tables[6][:, None, None]
    speed_y = own_tables[7][:, None, None]
    energy_field = in_bins.astype(jnp.float32).reshape(bins_each, column_count, LAT)[:, inverse]
    for substep in range(SUBSTEPS):
        widened = padded(energy_field, (("sec", 1),), 1)
        energy_field = wet_grid * advance(
            widened[:, 1:-1], widened[:, :-2], widened[:, 2:], speed_x, speed_y
        )
    leaving = energy_field[:, order_all].reshape(bins_each, column_count * LAT).astype(jnp.bfloat16)
    returned = lax.all_to_all(leaving, "dom", split_axis=1, concat_axis=0, tiled=True)
    new_spectrum = returned[:bin_count]
    own_stress = lax.dynamic_slice_in_dim(
        stress_store[:, inverse], dom_rank * block_count, block_count, 1
    )
    wave_stress = wet_mask[None, :] * own_stress.reshape(2, point_count)
    return (new_spectrum, wave_stress)


def solution(mesh):
    placed = (
        P(None, ("sec", "dom")),
        P(None, ("sec", "dom")),
        P(("sec", "dom")),
        P(("sec", "dom")),
    )
    return jax.shard_map(
        on_device,
        mesh=mesh,
        in_specs=placed,
        out_specs=(P(None, ("sec", "dom")), P(None, ("sec", "dom"))),
        check_vma=False,
    )
```

profile of v0, /device:TPU:0, one launch (start us, length us, event | category | flops | bytes accessed | tf_op | source)
XLA Modules:
  0.0 101.6 jit_solution(7459056079119182537)
XLA Ops:
  0.6 0.0 copy-start.2
  0.6 0.0 copy-start
  0.7 0.1 fusion.50
  1.5 0.0 copy-done.2
  1.5 0.6 dynamic-slice.9
  2.1 0.8 dynamic-update-slice.2
  2.8 10.6 %all-reduce.8 = s32[8]{0:T(128)S(1)} all-reduce(s32[8]{0:T(128)S(1)} %dynamic-update-slice.2), channel_id=1, replica_groups=mesh['sec'=4,'dom'=8] {'dom'}, use_global_device_ids=true, to_apply=%add.8 | all-reduce | flops 8 | bytes 64
  13.4 0.6 dynamic_slice.6
  15.3 9.4 %all-gather = f32[8,1,128]{2,1,0:T(1,128)S(1)} all-gather(f32[1,1,128]{2,1,0:T(1,128)} %bitcast.40), channel_id=1, replica_groups=mesh['sec'=4,'dom'=8] {'dom'}, dimensions={0}, use_global_device_ids=true | all-gather | bytes 4608 | tf_op jit(solution)/shard_map/all_gather | solution.py:131
  24.7 9.8 %all_gather.14 = f32[2,1024]{1,0:T(2,128)S(1)} all-gather(f32[2,128]{1,0:T(2,128)} %param.5), channel_id=1, replica_groups=mesh['sec'=4,'dom'=8] {'dom'}, dimensions={1}, use_global_device_ids=true | all-gather | bytes 9216 | tf_op jit(solution)/shard_map/all_gather | solution.py:130
  35.2 1.6 %fusion.38 = (f32[128]{0:T(128)S(1)}, f32[128]{0:T(128)S(1)}, f32[128]{0:T(128)S(1)}) fusion(bf16[1296,128]{1,0:T(8,128)(2,1)} %param.4, f32[1296]{0:T(1024)S(1)} %get-tuple-element.55, f32[1296]{0:T(1024)S(1)} %get-tuple-element.56, f32[1296]{0:T(1024)S(1)} %fusion.55), kind=kLoop, calls=%fused_computation.57 | loop fusion | flops 1160832 | bytes 348864 | tf_op jit(solution)/shard_map/reduce_sum | solution.py:72
  36.7 0.0 copy-done
  36.8 1.1 %fusion.37 = (f32[1296,128]{1,0:T(8,128)S(1)}, bf16[1296,128]{1,0:T(8,128)(2,1)S(1)}) fusion(bf16[1296,128]{1,0:T(8,128)(2,1)S(1)} %copy-done, f32[1296]{0:T(1024)S(1)} %get-tuple-element.55, f32[1296]{0:T(1024)S(1)} %get-tuple-element.58, f32[128]{0:T(128)S(1)} %get-tuple-element.50, f32[1296]{0:T(1024)S(1)} %get-tuple-element.59, ...), kind=kLoop, calls=%fused_computation.53 | loop fusion | flops 3815424 | bytes 1360768 | tf_op jit(solution)/shard_map/div | solution.py:78
  37.9 0.8 all_to_all.22
  38.7 3.4 %all-to-all-start = ((bf16[8,162,128]{2,1,0:T(8,128)(2,1)}), bf16[8,162,128]{2,1,0:T(8,128)(2,1)S(1)}, u32[]{:S(2)}, u32[]{:S(2)}) async-start(bf16[8,162,128]{2,1,0:T(8,128)(2,1)} %all_to_all.22), calls=%async_computation | async-start | bytes 688128 | tf_op jit(solution)/shard_map/all_to_all | solution.py:143
  42.1 0.1 negate_maximum_fusion
  42.2 0.1 broadcast_maximum_fusion.1
  42.3 0.6 scatter_custom_fusion
  42.9 0.1 abs_subtract_fusion
  43.0 10.6 %all-to-all-done = bf16[8,162,128]{2,1,0:T(8,128)(2,1)S(1)} async-done(((bf16[8,162,128]{2,1,0:T(8,128)(2,1)}), bf16[8,162,128]{2,1,0:T(8,128)(2,1)S(1)}, u32[]{:S(2)}, u32[]{:S(2)}) %all-to-all-start) | async-done | bytes 331808 | tf_op jit(solution)/shard_map/all_to_all | solution.py:143
  53.6 0.6 gather_fusion
  54.2 1.5 %collective-permute-start = (f32[162,1,128]{2,0,1:T(8,128)S(1)}, f32[162,1,128]{2,0,1:T(8,128)S(1)}, u32[]{:S(2)}, u32[]{:S(2)}) collective-permute-start(f32[162,1,128]{2,0,1:T(8,128)S(1)} %get-tuple-element.45), channel_id=1, source_target_pairs={{0,8},{8,16},{16,24},{24,0},{1,9},{9,17},{17,25},{25,1},{2,10},{10... | collective-permute-start | bytes 248840 | tf_op jit(solution)/shard_map/ppermute | solution.py:30
  55.8 1.4 %collective-permute-start.1 = (f32[162,1,128]{2,0,1:T(8,128)S(1)}, f32[162,1,128]{2,0,1:T(8,128)S(1)}, u32[]{:S(2)}, u32[]{:S(2)}) collective-permute-start(f32[162,1,128]{2,0,1:T(8,128)S(1)} %get-tuple-element.46), channel_id=1, source_target_pairs={{8,0},{16,8},{24,16},{0,24},{9,1},{17,9},{25,17},{1,25},{10,2},{18... | collective-permute-start | bytes 248840 | tf_op jit(solution)/shard_map/ppermute | solution.py:33
  57.2 0.2 fusion.73
  57.4 2.8 %collective-permute-done = f32[162,1,128]{2,0,1:T(8,128)S(1)} collective-permute-done((f32[162,1,128]{2,0,1:T(8,128)S(1)}, f32[162,1,128]{2,0,1:T(8,128)S(1)}, u32[]{:S(2)}, u32[]{:S(2)}) %collective-permute-start) | collective-permute-done | bytes 82976 | tf_op jit(solution)/shard_map/ppermute | solution.py:30
  60.2 0.6 collective-permute-done.1
  60.9 0.4 fusion.29
  61.3 1.8 %collective-permute-start.2 = (f32[162,1,128]{2,0,1:T(8,128)S(1)}, f32[162,1,128]{2,0,1:T(8,128)S(1)}, u32[]{:S(2)}, u32[]{:S(2)}) collective-permute-start(f32[162,1,128]{2,0,1:T(8,128)S(1)} %get-tuple-element.41), channel_id=1, source_target_pairs={{0,8},{8,16},{16,24},{24,0},{1,9},{9,17},{17,25},{25,1},{2,10},{10... | collective-permute-start | bytes 248840 | tf_op jit(solution)/shard_map/ppermute | solution.py:30
  63.1 1.2 %collective-permute-start.3 = (f32[162,1,128]{2,0,1:T(8,128)S(1)}, f32[162,1,128]{2,0,1:T(8,128)S(1)}, u32[]{:S(2)}, u32[]{:S(2)}) collective-permute-start(f32[162,1,128]{2,0,1:T(8,128)S(1)} %get-tuple-element.42), channel_id=1, source_target_pairs={{8,0},{16,8},{24,16},{0,24},{9,1},{17,9},{25,17},{1,25},{10,2},{18... | collective-permute-start | bytes 248840 | tf_op jit(solution)/shard_map/ppermute | solution.py:33
  64.2 0.2 fusion.71
  64.5 2.2 %collective-permute-done.2 = f32[162,1,128]{2,0,1:T(8,128)S(1)} collective-permute-done((f32[162,1,128]{2,0,1:T(8,128)S(1)}, f32[162,1,128]{2,0,1:T(8,128)S(1)}, u32[]{:S(2)}, u32[]{:S(2)}) %collective-permute-start.2) | collective-permute-done | bytes 82976 | tf_op jit(solution)/shard_map/ppermute | solution.py:30
  66.7 0.9 collective-permute-done.3
  67.6 0.4 fusion.22
  68.0 1.5 %collective-permute-start.4 = (f32[162,1,128]{2,0,1:T(8,128)S(1)}, f32[162,1,128]{2,0,1:T(8,128)S(1)}, u32[]{:S(2)}, u32[]{:S(2)}) collective-permute-start(f32[162,1,128]{2,0,1:T(8,128)S(1)} %get-tuple-element.37), channel_id=1, source_target_pairs={{0,8},{8,16},{16,24},{24,0},{1,9},{9,17},{17,25},{25,1},{2,10},{10... | collective-permute-start | bytes 248840 | tf_op jit(solution)/shard_map/ppermute | solution.py:30
  69.5 1.4 %collective-permute-start.5 = (f32[162,1,128]{2,0,1:T(8,128)S(1)}, f32[162,1,128]{2,0,1:T(8,128)S(1)}, u32[]{:S(2)}, u32[]{:S(2)}) collective-permute-start(f32[162,1,128]{2,0,1:T(8,128)S(1)} %get-tuple-element.38), channel_id=1, source_target_pairs={{8,0},{16,8},{24,16},{0,24},{9,1},{17,9},{25,17},{1,25},{10,2},{18... | collective-permute-start | bytes 248840 | tf_op jit(solution)/shard_map/ppermute | solution.py:33
  71.0 0.2 fusion.69
  71.2 2.2 %collective-permute-done.4 = f32[162,1,128]{2,0,1:T(8,128)S(1)} collective-permute-done((f32[162,1,128]{2,0,1:T(8,128)S(1)}, f32[162,1,128]{2,0,1:T(8,128)S(1)}, u32[]{:S(2)}, u32[]{:S(2)}) %collective-permute-start.4) | collective-permute-done | bytes 82976 | tf_op jit(solution)/shard_map/ppermute | solution.py:30
  73.4 1.2 %collective-permute-done.5 = f32[162,1,128]{2,0,1:T(8,128)S(1)} collective-permute-done((f32[162,1,128]{2,0,1:T(8,128)S(1)}, f32[162,1,128]{2,0,1:T(8,128)S(1)}, u32[]{:S(2)}, u32[]{:S(2)}) %collective-permute-start.5) | collective-permute-done | bytes 82976 | tf_op jit(solution)/shard_map/ppermute | solution.py:33
  74.6 0.4 fusion.15
  75.0 1.2 %collective-permute-start.6 = (f32[162,1,128]{2,0,1:T(8,128)S(1)}, f32[162,1,128]{2,0,1:T(8,128)S(1)}, u32[]{:S(2)}, u32[]{:S(2)}) collective-permute-start(f32[162,1,128]{2,0,1:T(8,128)S(1)} %get-tuple-element.33), channel_id=1, source_target_pairs={{0,8},{8,16},{16,24},{24,0},{1,9},{9,17},{17,25},{25,1},{2,10},{10... | collective-permute-start | bytes 248840 | tf_op jit(solution)/shard_map/ppermute | solution.py:30
  76.2 1.8 %collective-permute-start.7 = (f32[162,1,128]{2,0,1:T(8,128)S(1)}, f32[162,1,128]{2,0,1:T(8,128)S(1)}, u32[]{:S(2)}, u32[]{:S(2)}) collective-permute-start(f32[162,1,128]{2,0,1:T(8,128)S(1)} %get-tuple-element.34), channel_id=1, source_target_pairs={{8,0},{16,8},{24,16},{0,24},{9,1},{17,9},{25,17},{1,25},{10,2},{18... | collective-permute-start | bytes 248840 | tf_op jit(solution)/shard_map/ppermute | solution.py:33
  78.0 0.2 fusion.67
  78.3 2.2 %collective-permute-done.6 = f32[162,1,128]{2,0,1:T(8,128)S(1)} collective-permute-done((f32[162,1,128]{2,0,1:T(8,128)S(1)}, f32[162,1,128]{2,0,1:T(8,128)S(1)}, u32[]{:S(2)}, u32[]{:S(2)}) %collective-permute-start.6) | collective-permute-done | bytes 82976 | tf_op jit(solution)/shard_map/ppermute | solution.py:30
  80.5 0.6 collective-permute-done.7
  81.1 0.4 fusion.8
  81.5 1.3 %gather_fusion.1 = bf16[8,162,128]{2,1,0:T(8,128)(2,1)} fusion(bf16[162,8,128]{2,0,1:T(8,128)(2,1)S(1)} %fusion.8, s32[1024]{0:T(1024)S(1)} %pad_clamp_fusion), kind=kCustom, calls=%fused_computation.1 | custom fusion | bytes 663584 | tf_op jit(solution)/shard_map/gather | solution.py:157
  82.8 3.4 %all-to-all-start.1 = ((bf16[162,8,128]{2,0,1:T(8,128)(2,1)}), bf16[162,8,128]{2,0,1:T(8,128)(2,1)S(1)}, u32[]{:S(2)}, u32[]{:S(2)}) async-start(bf16[162,8,128]{2,0,1:T(8,128)(2,1)} %bitcast.25), calls=%async_computation.1 | async-start | bytes 688128 | tf_op jit(solution)/shard_map/all_to_all | solution.py:158
  86.2 0.4 multiply_reduce_fusion.1
  86.7 12.9 %all_gather.15 = f32[2,1024]{1,0:T(2,128)S(1)} all-gather(f32[2,128]{1,0:T(2,128)S(1)} %maximum_multiply_fusion.1), channel_id=1, replica_groups=mesh['sec'=4,'dom'=8] {'dom'}, dimensions={1}, use_global_device_ids=true | all-gather | bytes 9216 | tf_op jit(solution)/shard_map/all_gather | solution.py:146
  99.5 0.0 copy-start.1
  99.5 0.6 gather_fusion.2
  100.1 0.1 copy-done.1
  100.2 0.6 bitcast_multiply_fusion
  100.7 0.0 all-to-all-done.1
  100.8 0.8 all_to_all.26
  (20 shorter events, 0.3 us)
Async XLA Ops:
  0.6 0.8 copy-start.2
  0.6 36.1 %copy-start = (bf16[1296,128]{1,0:T(8,128)(2,1)S(1)}, bf16[1296,128]{1,0:T(8,128)(2,1)}, u32[]{:S(2)}) copy-start(bf16[1296,128]{1,0:T(8,128)(2,1)} %param.4) | copy-start | bytes 995332
  38.7 14.9 %all-to-all-start = ((bf16[8,162,128]{2,1,0:T(8,128)(2,1)}), bf16[8,162,128]{2,1,0:T(8,128)(2,1)S(1)}, u32[]{:S(2)}, u32[]{:S(2)}) async-start(bf16[8,162,128]{2,1,0:T(8,128)(2,1)} %all_to_all.22), calls=%async_computation | async-start | bytes 688128 | tf_op jit(solution)/shard_map/all_to_all | solution.py:143
  54.2 6.0 %collective-permute-start = (f32[162,1,128]{2,0,1:T(8,128)S(1)}, f32[162,1,128]{2,0,1:T(8,128)S(1)}, u32[]{:S(2)}, u32[]{:S(2)}) collective-permute-start(f32[162,1,128]{2,0,1:T(8,128)S(1)} %get-tuple-element.45), channel_id=1, source_target_pairs={{0,8},{8,16},{16,24},{24,0},{1,9},{9,17},{17,25},{25,1},{2,10},{10... | collective-permute-start | bytes 248840 | tf_op jit(solution)/shard_map/ppermute | solution.py:30
  55.8 5.1 %collective-permute-start.1 = (f32[162,1,128]{2,0,1:T(8,128)S(1)}, f32[162,1,128]{2,0,1:T(8,128)S(1)}, u32[]{:S(2)}, u32[]{:S(2)}) collective-permute-start(f32[162,1,128]{2,0,1:T(8,128)S(1)} %get-tuple-element.46), channel_id=1, source_target_pairs={{8,0},{16,8},{24,16},{0,24},{9,1},{17,9},{25,17},{1,25},{10,2},{18... | collective-permute-start | bytes 248840 | tf_op jit(solution)/shard_map/ppermute | solution.py:33
  61.3 5.4 %collective-permute-start.2 = (f32[162,1,128]{2,0,1:T(8,128)S(1)}, f32[162,1,128]{2,0,1:T(8,128)S(1)}, u32[]{:S(2)}, u32[]{:S(2)}) collective-permute-start(f32[162,1,128]{2,0,1:T(8,128)S(1)} %get-tuple-element.41), channel_id=1, source_target_pairs={{0,8},{8,16},{16,24},{24,0},{1,9},{9,17},{17,25},{25,1},{2,10},{10... | collective-permute-start | bytes 248840 | tf_op jit(solution)/shard_map/ppermute | solution.py:30
  63.1 4.5 %collective-permute-start.3 = (f32[162,1,128]{2,0,1:T(8,128)S(1)}, f32[162,1,128]{2,0,1:T(8,128)S(1)}, u32[]{:S(2)}, u32[]{:S(2)}) collective-permute-start(f32[162,1,128]{2,0,1:T(8,128)S(1)} %get-tuple-element.42), channel_id=1, source_target_pairs={{8,0},{16,8},{24,16},{0,24},{9,1},{17,9},{25,17},{1,25},{10,2},{18... | collective-permute-start | bytes 248840 | tf_op jit(solution)/shard_map/ppermute | solution.py:33
  68.0 5.4 %collective-permute-start.4 = (f32[162,1,128]{2,0,1:T(8,128)S(1)}, f32[162,1,128]{2,0,1:T(8,128)S(1)}, u32[]{:S(2)}, u32[]{:S(2)}) collective-permute-start(f32[162,1,128]{2,0,1:T(8,128)S(1)} %get-tuple-element.37), channel_id=1, source_target_pairs={{0,8},{8,16},{16,24},{24,0},{1,9},{9,17},{17,25},{25,1},{2,10},{10... | collective-permute-start | bytes 248840 | tf_op jit(solution)/shard_map/ppermute | solution.py:30
  69.5 5.1 %collective-permute-start.5 = (f32[162,1,128]{2,0,1:T(8,128)S(1)}, f32[162,1,128]{2,0,1:T(8,128)S(1)}, u32[]{:S(2)}, u32[]{:S(2)}) collective-permute-start(f32[162,1,128]{2,0,1:T(8,128)S(1)} %get-tuple-element.38), channel_id=1, source_target_pairs={{8,0},{16,8},{24,16},{0,24},{9,1},{17,9},{25,17},{1,25},{10,2},{18... | collective-permute-start | bytes 248840 | tf_op jit(solution)/shard_map/ppermute | solution.py:33
  75.0 5.4 %collective-permute-start.6 = (f32[162,1,128]{2,0,1:T(8,128)S(1)}, f32[162,1,128]{2,0,1:T(8,128)S(1)}, u32[]{:S(2)}, u32[]{:S(2)}) collective-permute-start(f32[162,1,128]{2,0,1:T(8,128)S(1)} %get-tuple-element.33), channel_id=1, source_target_pairs={{0,8},{8,16},{16,24},{24,0},{1,9},{9,17},{17,25},{25,1},{2,10},{10... | collective-permute-start | bytes 248840 | tf_op jit(solution)/shard_map/ppermute | solution.py:30
  76.2 4.8 %collective-permute-start.7 = (f32[162,1,128]{2,0,1:T(8,128)S(1)}, f32[162,1,128]{2,0,1:T(8,128)S(1)}, u32[]{:S(2)}, u32[]{:S(2)}) collective-permute-start(f32[162,1,128]{2,0,1:T(8,128)S(1)} %get-tuple-element.34), channel_id=1, source_target_pairs={{8,0},{16,8},{24,16},{0,24},{9,1},{17,9},{25,17},{1,25},{10,2},{18... | collective-permute-start | bytes 248840 | tf_op jit(solution)/shard_map/ppermute | solution.py:33
  82.8 18.0 %all-to-all-start.1 = ((bf16[162,8,128]{2,0,1:T(8,128)(2,1)}), bf16[162,8,128]{2,0,1:T(8,128)(2,1)S(1)}, u32[]{:S(2)}, u32[]{:S(2)}) async-start(bf16[162,8,128]{2,0,1:T(8,128)(2,1)} %bitcast.25), calls=%async_computation.1 | async-start | bytes 688128 | tf_op jit(solution)/shard_map/all_to_all | solution.py:158
  99.5 0.7 copy-start.1
where the time goes:
time: 102 us
  blocking collectives  42.6 us (42%)
  waiting for transfers between devices  23.3 us (23%)
  starting transfers between devices  18.8 us (18%)
  local copies, waits for them, and re-layouts  7.79 us (8%)
  other arithmetic  5.55 us (5%)
  between operations  3.5 us (3%)
    all_gather x1, blocking collectives, on_device(): lax.all_gather(stress_coef * momentum, 'dom', axis=1, tiled=True)  12.9 us
    unnamed x1, blocking collectives  10.6 us
    all_to_all x1, waiting for transfers between devices, on_device(): lax.all_to_all(jnp.pad(renewed, ((0, padding), (0, 0))), 'dom', split_axi...  10.6 us
    all_gather x1, blocking collectives, on_device(): lax.all_gather(surface_wind, 'dom', axis=1, tiled=True)  9.78 us
    ppermute x4, waiting for transfers between devices, padded(): lax.ppermute(lax.slice_in_dim(block, block.shape[dim] - width, None, axis...  9.44 us
    all_gather x1, blocking collectives, on_device(): lax.all_gather(wet_mask, 'dom', axis=0, tiled=True)  9.36 us
    ppermute x4, starting transfers between devices, padded(): lax.ppermute(lax.slice_in_dim(block, block.shape[dim] - width, None, axis...  6.1 us
    ppermute x4, starting transfers between devices, padded(): lax.ppermute(lax.slice_in_dim(block, 0, width, axis=dim), axis, backward)  5.8 us
  transfers between devices with their start and end apart: 10, of which 9 were waited for; matrix products, arithmetic and copies ran while one was open for 3% of the time, Pallas kernels for 0%

commit v1 on v0

v1 whole, which is shorter than its diff:
```python
import functools
import math

import jax
import jax.numpy as jnp
import numpy as np
from jax import lax
from jax.experimental import pallas as pl
from jax.experimental.pallas import tpu as pltpu
from jax.sharding import PartitionSpec as P

NF = 36
ND = 36
BINS = NF * ND
LAT = 128
SUBSTEPS = 4

gravity = 9.81
base_freq = 0.035
freq_growth = 1.1
wind_rate = 0.015
dissip_rate = 0.008
steep_ref = 3.0
stress_coef = 0.01
courant = 0.62

AXES = ("sec", "dom")
TILE = 8
GROUP_TILES = 9
BF = jnp.bfloat16
F32 = jnp.float32

FREQ = np.arange(NF, dtype=np.float64)
SIGMA = 2.0 * math.pi * base_freq * freq_growth**FREQ
WAVENUM = SIGMA * SIGMA / gravity
SPEED = gravity / SIGMA
AREA = 0.1 * SIGMA * (2.0 * math.pi / ND)
THETA = 2.0 * math.pi * np.arange(ND, dtype=np.float64) / ND
COS = np.cos(THETA)
SIN = np.sin(THETA)


def vmem():
    return pl.BlockSpec(memory_space=pltpu.VMEM)


def smem():
    return pl.BlockSpec(memory_space=pltpu.SMEM)


def layout(devices):
    each = BINS // devices
    rows = -(-(each + TILE) // 16) * 16
    return each, rows - TILE, rows


def device_tables(devices):
    each, kept, rows = layout(devices)
    table = np.zeros((devices, 8, rows), np.float64)
    for device in range(devices):
        bins = np.full((rows,), -1)
        bins[:each] = device * each + np.arange(each)
        if devices * each + device < BINS:
            bins[kept] = devices * each + device
        real = bins >= 0
        i, j = np.maximum(bins, 0) // ND, np.maximum(bins, 0) % ND
        scale = wind_rate * SIGMA[i]
        travel = courant * freq_growth ** (-i.astype(np.float64))
        cx, cy = travel * COS[j], travel * SIN[j]
        values = (
            scale * 1.2 / SPEED[i] * COS[j],
            scale * 1.2 / SPEED[i] * SIN[j],
            scale,
            1.0 - np.abs(cx) - np.abs(cy),
            np.maximum(cx, 0.0),
            np.maximum(-cx, 0.0),
            np.maximum(cy, 0.0),
            np.maximum(-cy, 0.0),
        )
        for row, value in enumerate(values):
            table[device, row] = np.where(real, value, 0.0)
    return table.astype(np.float32)


def split(value):
    high = value.astype(BF)
    return high.astype(F32), (value - high.astype(F32)).astype(BF).astype(F32)


def row_ids():
    return lax.broadcasted_iota(jnp.int32, (TILE, LAT), 0)


def stack_rows(rows):
    ids = row_ids()
    tile = jnp.zeros((TILE, LAT), F32)
    for r, row in enumerate(rows):
        if row is not None:
            tile = jnp.where(ids == r, jnp.broadcast_to(row, (TILE, LAT)), tile)
    return tile


def tile_freqs(t):
    return (TILE * t) // ND, (TILE * t + TILE - 1) // ND


def decayed_tiles(spectrum_ref):
    ids = row_ids()
    upper = ids < TILE // 2
    tiles = []
    for pair in range(BINS // 16):
        both = spectrum_ref[16 * pair : 16 * pair + 16, :].astype(F32)
        tiles += [both[:TILE], both[TILE:]]
    sums = [jnp.zeros((TILE, LAT), F32) for _ in range(3)]
    for group in range(NF // 2):
        nine = tiles[GROUP_TILES * group : GROUP_TILES * (group + 1)]
        low = (nine[0] + nine[1]) + (nine[2] + nine[3]) + jnp.where(upper, nine[4], 0.0)
        high = (nine[5] + nine[6]) + (nine[7] + nine[8]) + jnp.where(upper, 0.0, nine[4])
        for i, part in ((2 * group, low), (2 * group + 1, high)):
            weights = (AREA[i], AREA[i] / SIGMA[i], AREA[i] / math.sqrt(WAVENUM[i]))
            sums = [s + float(np.float32(w)) * part for s, w in zip(sums, weights)]
    moments = [jnp.broadcast_to(jnp.sum(s, axis=0, keepdims=True), (TILE, LAT)) for s in sums]
    mean_freq = moments[0] / moments[1]
    mean_wavenum = (moments[0] / moments[2]) ** 2
    steepness = moments[0] * mean_wavenum * mean_wavenum
    strength = mean_freq * (steepness / steep_ref) ** 2
    inverse = 1.0 / mean_wavenum
    factors = []
    for i in range(NF):
        ratio = float(np.float32(WAVENUM[i])) * inverse
        factors.append(jnp.exp(-dissip_rate * (strength * (0.5 * ratio + 0.5 * ratio * ratio))))
    out = []
    for t, tile in enumerate(tiles):
        first, last = tile_freqs(t)
        factor = factors[first]
        if last != first:
            factor = jnp.where(upper, factor, factors[last])
        out.append(tile * factor)
    return out


def shared_tile(wind_ref, wet_ref, order):
    east, north, wet = split(wind_ref[0:1, :]), split(wind_ref[1:2, :]), split(wet_ref[0:1, :])
    column = jnp.full((1, LAT), order, jnp.int32).astype(F32)
    return stack_rows([None, *east, *north, *wet, column])


def pack_kernel(devices, order_ref, spectrum_ref, wind_ref, wet_ref, out_ref):
    each, kept, rows = layout(devices)
    tiles = decayed_tiles(spectrum_ref)
    shared = shared_tile(wind_ref, wet_ref, order_ref[0])
    first = row_ids() == 0
    left = BINS - devices * each
    per = each // TILE
    for d in range(devices):
        last = shared
        if d < left:
            spare = tiles[per * devices + d // TILE]
            row = spare[d % TILE : d % TILE + 1]
            last = jnp.where(first, jnp.broadcast_to(row, (TILE, LAT)), shared)
        chunk = jnp.concatenate(tiles[per * d : per * (d + 1)] + [last], axis=0)
        out_ref[d] = chunk.astype(BF)


def loose_kernel(order_ref, spectrum_ref, wind_ref, wet_ref, out_ref, shared_ref):
    tiles = decayed_tiles(spectrum_ref)
    for pair in range(BINS // 16):
        both = jnp.concatenate(tiles[2 * pair : 2 * pair + 2], axis=0)
        out_ref[16 * pair : 16 * pair + 16, :] = both.astype(BF)
    shared_ref[...] = shared_tile(wind_ref, wet_ref, order_ref[0])


def packed(devices, block_order, spectrum, surface_wind, wet):
    each, kept, rows = layout(devices)
    shape = jax.ShapeDtypeStruct((devices, rows, LAT), BF)
    params = pltpu.CompilerParams(vmem_limit_bytes=24 << 20)
    in_specs = [smem(), vmem(), vmem(), vmem()]
    if each == kept:
        return pl.pallas_call(
            functools.partial(pack_kernel, devices),
            out_shape=shape,
            in_specs=in_specs,
            out_specs=vmem(),
            compiler_params=params,
        )(block_order, spectrum, surface_wind, wet)
    decayed, shared = pl.pallas_call(
        loose_kernel,
        out_shape=(
            jax.ShapeDtypeStruct((BINS, LAT), BF),
            jax.ShapeDtypeStruct((TILE, LAT), F32),
        ),
        in_specs=in_specs,
        out_specs=(vmem(), vmem()),
        compiler_params=params,
    )(block_order, spectrum, surface_wind, wet)
    main = decayed[: devices * each].reshape(devices, each, LAT)
    main = jnp.pad(main, ((0, 0), (0, kept - each), (0, 0)))
    spare = decayed[devices * each :]
    spare = jnp.pad(spare, ((0, devices - spare.shape[0]), (0, 0)))[:, None]
    common = jnp.broadcast_to(shared[1:].astype(BF)[None], (devices, TILE - 1, LAT))
    return jnp.concatenate([main, spare, common], axis=1)


def own_stress(spectrum_ref, angles_ref, east, north):
    upper = row_ids() < TILE // 2
    cosines = [angles_ref[0, TILE * p : TILE * (p + 1), :] for p in range(GROUP_TILES)]
    sines = [angles_ref[1, TILE * p : TILE * (p + 1), :] for p in range(GROUP_TILES)]
    along = [c * east + s * north for c, s in zip(cosines, sines)]
    totals = [jnp.zeros((TILE, LAT), F32) for _ in range(GROUP_TILES)]

    def constant(values, first, last):
        low, high = float(np.float32(values[first])), float(np.float32(values[last]))
        return low if first == last else jnp.where(upper, low, high)

    for pair in range(BINS // 16):
        both = spectrum_ref[16 * pair : 16 * pair + 16, :].astype(F32)
        for half in range(2):
            t = 2 * pair + half
            p = t % GROUP_TILES
            tile = both[TILE * half : TILE * (half + 1)]
            slope = constant(1.2 / SPEED, *tile_freqs(t))
            weight = constant(stress_coef * AREA * SIGMA / SPEED, *tile_freqs(t))
            grown = jnp.maximum(0.0, slope * along[p] - 1.0)
            totals[p] = totals[p] + (weight * tile) * grown
    return [
        jnp.sum(sum(a * b for a, b in zip(parts, totals)), axis=0, keepdims=True)
        for parts in (cosines, sines)
    ]


def spread_kernel(
    devices, section, order_ref, recv_ref, spectrum_ref, table_ref, angles_ref, out_ref,
    field_a, field_b, wet_ref, order_vmem, order_smem, column_smem, slot_smem, sem,
):
    each, kept, rows = layout(devices)
    ids = row_ids()
    lane = lax.broadcasted_iota(jnp.int32, (TILE, LAT), 1)
    blocks = -(-devices // LAT)
    for block in range(blocks):

        def place(s, tile, block=block):
            here = recv_ref[block * LAT + s, kept : kept + TILE, :].astype(F32)
            return jnp.where(lane == s, here, tile)

        count = min(LAT, devices - block * LAT)
        orders = lax.fori_loop(0, count, place, jnp.zeros((TILE, LAT), F32), unroll=8)
        order_vmem[block] = orders.astype(jnp.int32)
    copy = pltpu.make_async_copy(order_vmem, order_smem, sem)
    copy.start()
    copy.wait()

    def number(s, carry):
        column = s // section * section + order_smem[s // LAT, TILE - 1, s % LAT]
        column_smem[s] = column
        slot_smem[column] = s
        return carry

    lax.fori_loop(0, devices, number, 0, unroll=8)

    def weather(column):
        tile = recv_ref[column, kept : kept + TILE, :].astype(F32)
        east, north = tile[1:2] + tile[2:3], tile[3:4] + tile[4:5]
        return east, north, tile[5:6] + tile[6:7]

    me = lax.axis_index("sec") * section + lax.axis_index("dom")
    stress = own_stress(spectrum_ref, angles_ref, *weather(me // section * section + order_ref[0])[:2])
    parts = split(stress[0]) + split(stress[1])
    column_row = jnp.full((1, LAT), order_ref[0], jnp.int32).astype(F32)
    ending = stack_rows([None, *parts, None, None, column_row])

    def renew(column, carry):
        east, north, wet = weather(column)
        wet_ref[column] = jnp.broadcast_to(wet, (TILE, LAT))
        energy = recv_ref[slot_smem[column]].astype(F32)
        push = jnp.exp(
            jnp.maximum(0.0, table_ref[0] * east + table_ref[1] * north - table_ref[2])
        )
        field_a[column] = (wet * energy * push).astype(BF).astype(F32)
        return carry

    lax.fori_loop(0, devices, renew, 0, unroll=2)

    def moved(source, column):
        here = source[column]
        west = source[jnp.where(column == 0, devices - 1, column - 1)]
        east = source[jnp.where(column == devices - 1, 0, column + 1)]
        total = table_ref[3] * here + table_ref[4] * west + table_ref[5] * east
        total = total + table_ref[6] * pltpu.roll(here, 1, 1)
        total = total + table_ref[7] * pltpu.roll(here, LAT - 1, 1)
        return wet_ref[column, 0:1, :] * total

    fields = (field_a, field_b)
    for substep in range(SUBSTEPS - 1):
        source, target = fields[substep % 2], fields[(substep + 1) % 2]

        def step(column, carry, source=source, target=target):
            target[column] = moved(source, column)
            return carry

        lax.fori_loop(0, devices, step, 0, unroll=2)
    source = fields[(SUBSTEPS - 1) % 2]

    def finish(column, carry):
        total = moved(source, column)
        last = jnp.where(ids == 0, total[kept:], ending)
        out_ref[slot_smem[column]] = jnp.concatenate([total[:kept], last], axis=0).astype(BF)
        return carry

    lax.fori_loop(0, devices, finish, 0, unroll=2)


def spread(devices, section, block_order, received, spectrum, table):
    each, kept, rows = layout(devices)
    angle = np.arange(GROUP_TILES * TILE) % ND
    angles = np.broadcast_to(
        np.stack([COS[angle], SIN[angle]]).astype(np.float32)[:, :, None],
        (2, GROUP_TILES * TILE, LAT),
    )
    blocks = -(-devices // LAT)
    return pl.pallas_call(
        functools.partial(spread_kernel, devices, section),
        out_shape=jax.ShapeDtypeStruct((devices, rows, LAT), BF),
        in_specs=[smem(), vmem(), vmem(), vmem(), vmem()],
        out_specs=vmem(),
        scratch_shapes=[
            pltpu.VMEM((devices, rows, LAT), F32),
            pltpu.VMEM((devices, rows, LAT), F32),
            pltpu.VMEM((devices, TILE, LAT), F32),
            pltpu.VMEM((blocks, TILE, LAT), jnp.int32),
            pltpu.SMEM((blocks, TILE, LAT), jnp.int32),
            pltpu.SMEM((devices,), jnp.int32),
            pltpu.SMEM((devices,), jnp.int32),
            pltpu.SemaphoreType.DMA,
        ],
        compiler_params=pltpu.CompilerParams(vmem_limit_bytes=32 << 20),
    )(block_order, received, spectrum, table, jnp.asarray(angles))


def collect(devices, section, returned_ref, wet_ref, stress_ref):
    each, kept, rows = layout(devices)
    base = lax.axis_index("sec") * section
    rank = lax.axis_index("dom").astype(F32)

    def pick(s, total):
        tile = returned_ref[base + s, kept : kept + TILE, :].astype(F32)
        mine = jnp.broadcast_to(tile[TILE - 1 : TILE] == rank, (TILE, LAT))
        return jnp.where(mine, tile, total)

    tile = lax.fori_loop(0, section, pick, jnp.zeros((TILE, LAT), F32), unroll=8)
    wet = wet_ref[0:1, :]
    stress_ref[0:1, :] = wet * (tile[1:2] + tile[2:3])
    stress_ref[1:2, :] = wet * (tile[3:4] + tile[4:5])


def unpack_kernel(devices, section, returned_ref, wet_ref, out_ref, stress_ref):
    each, kept, rows = layout(devices)
    left = BINS - devices * each
    for pair in range(devices // 2):
        both = [returned_ref[2 * pair + half].astype(F32)[:each] for half in range(2)]
        out_ref[2 * each * pair : 2 * each * (pair + 1), :] = jnp.concatenate(both, axis=0).astype(BF)
    spare = []
    for tile in range(left // TILE):
        heads = [returned_ref[TILE * tile + r].astype(F32)[kept : kept + 1] for r in range(TILE)]
        spare.append(stack_rows(heads))
    out_ref[devices * each :, :] = jnp.concatenate(spare, axis=0).astype(BF)
    collect(devices, section, returned_ref, wet_ref, stress_ref)


def unpacked(devices, section, returned, wet):
    each, kept, rows = layout(devices)
    left = BINS - devices * each
    stress_shape = jax.ShapeDtypeStruct((2, LAT), F32)
    params = pltpu.CompilerParams(vmem_limit_bytes=24 << 20)
    if each == kept and devices % 2 == 0 and each % TILE == 0 and left % 16 == 0:
        return pl.pallas_call(
            functools.partial(unpack_kernel, devices, section),
            out_shape=(jax.ShapeDtypeStruct((BINS, LAT), BF), stress_shape),
            in_specs=[vmem(), vmem()],
            out_specs=(vmem(), vmem()),
            compiler_params=params,
        )(returned, wet)
    stress = pl.pallas_call(
        functools.partial(collect, devices, section),
        out_shape=stress_shape,
        in_specs=[vmem(), vmem()],
        out_specs=vmem(),
        compiler_params=params,
    )(returned, wet)
    main = returned[:, :each].reshape(devices * each, LAT)
    return jnp.concatenate([main, returned[:left, kept]], axis=0), stress


def on_device(devices, section, spectrum, surface_wind, wet_mask, block_order):
    wet = wet_mask.reshape(1, LAT)
    each, kept, rows = layout(devices)
    me = lax.axis_index(AXES)
    numbers = lax.dynamic_index_in_dim(jnp.asarray(device_tables(devices)), me, 0, keepdims=False)
    table = jnp.broadcast_to(numbers[:, :, None], (8, rows, LAT))
    lat = jnp.arange(LAT)
    which = jnp.arange(8)[:, None, None]
    edge = ((which == 6) & (lat == 0)) | ((which == 7) & (lat == LAT - 1))
    table = jnp.where(edge, 0.0, table)
    sending = packed(devices, block_order, spectrum, surface_wind, wet)
    received = lax.all_to_all(sending, AXES, split_axis=0, concat_axis=0, tiled=True)
    leaving = spread(devices, section, block_order, received, spectrum, table)
    returned = lax.all_to_all(leaving, AXES, split_axis=0, concat_axis=0, tiled=True)
    return unpacked(devices, section, returned, wet)


def solution(mesh):
    section = mesh.shape["dom"]
    devices = mesh.shape["sec"] * section
    placed = (P(None, AXES), P(None, AXES), P(AXES), P(AXES))
    return jax.shard_map(
        functools.partial(on_device, devices, section),
        mesh=mesh,
        in_specs=placed,
        out_specs=(P(None, AXES), P(None, AXES)),
        check_vma=False,
    )
```

time: 102 us -> 49.6 us (0.49)
  blocking collectives: 42.6 us -> 15.6 us
  starting transfers between devices: 18.8 us -> 7.3 us
  waiting for transfers between devices: 23.3 us -> 12.6 us
  Pallas kernels: 0 us -> 9.83 us
  local copies, waits for them, and re-layouts: 7.79 us -> 2.43 us
  other arithmetic: 5.55 us -> 0.2 us
  between operations: 3.5 us -> 1.35 us
    all_gather x3 -> x0, blocking collectives: 32 us -> none  [the longest x1 12.9 us: on_device(): lax.all_gather(stress_coef * momentum, 'dom', axis=1, tiled=True)]
    all_to_all x0 -> x1, blocking collectives: none -> 15.6 us  [on_device(): lax.all_to_all(leaving, AXES, split_axis=0, concat_axis=0, tiled=True)]
    ppermute x8 -> x0, waiting for transfers between devices: 12.8 us -> none  [the longest x4 9.44 us: padded(): lax.ppermute(lax.slice_in_dim(block, block.shape[dim] - width, None, axis...]
    ppermute x8 -> x0, starting transfers between devices: 11.9 us -> none  [the longest x4 6.1 us: padded(): lax.ppermute(lax.slice_in_dim(block, block.shape[dim] - width, None, axis...]
    unnamed x1 -> x0, blocking collectives: 10.6 us -> none
    pallas_call x0 -> x3, Pallas kernels: none -> 9.83 us  [the longest x1 8.08 us: spread(): pl.pallas_call(functools.partial(spread_kernel, devices, section), out_sh...]
    gather x3 -> x0, local copies, waits for them, and re-layouts: 2.49 us -> none  [the longest x1 1.33 us: on_device(): energy_field[:, order_all].reshape(bins_each, column_count * LAT)]
    mul x7 -> x0, other arithmetic: 2.09 us -> none  [the longest x4 1.5 us: on_device(): wet_grid * advance(widened[:, 1:-1], widened[:, :-2], widened[:, 2:], spe...]
  transfers between devices with their start and end apart: 10 -> 1, of which waited for: 9 -> 1; matrix products, arithmetic and copies ran while one was open for 3% -> 2% of each run, Pallas kernels for 0% -> 0%
where the time goes in v1:
time: 49.6 us; the launch traced here: 49.3 us
  blocking collectives  15.6 us (31%)
  waiting for transfers between devices  12.6 us (25%)
  Pallas kernels  9.83 us (20%)
  starting transfers between devices  7.3 us (15%)
  local copies, waits for them, and re-layouts  2.43 us (5%)
  between operations  1.35 us (3%)
    all_to_all x1, blocking collectives, on_device(): lax.all_to_all(leaving, AXES, split_axis=0, concat_axis=0, tiled=True)  15.6 us
    all_to_all x1, waiting for transfers between devices, on_device(): lax.all_to_all(sending, AXES, split_axis=0, concat_axis=0, tiled=True)  12.6 us
    pallas_call x1, Pallas kernels, spread(): pl.pallas_call(functools.partial(spread_kernel, devices, section), out_sh...  8.08 us
    all_to_all x1, starting transfers between devices, on_device(): lax.all_to_all(sending, AXES, split_axis=0, concat_axis=0, tiled=True)  7.3 us
    unnamed x10, local copies, waits for them, and re-layouts  1.66 us
  transfers between devices with their start and end apart: 1, of which 1 were waited for; matrix products, arithmetic and copies ran while one was open for 2% of the time, Pallas kernels for 0%

profile of v1, /device:TPU:0, one launch (start us, length us, event | category | flops | bytes accessed | tf_op | source)
XLA Modules:
  0.0 49.3 jit_solution(10543174281102193062)
XLA Ops:
  1.3 0.0 copy-start.2
  1.3 0.0 copy-start.3
  1.3 0.6 %copy-done.2 = f32[128]{0:T(128)S(1)} copy-done((f32[128]{0:T(128)S(1)}, f32[128]{0:T(128)}, u32[]{:S(2)}) %copy-start.2) | copy-done | bytes 536
  1.9 0.0 copy-done.3
  2.0 0.0 copy-start
  2.0 1.0 %copy-done = bf16[1296,128]{1,0:T(8,128)(2,1)S(1)} copy-done((bf16[1296,128]{1,0:T(8,128)(2,1)S(1)}, bf16[1296,128]{1,0:T(8,128)(2,1)}, u32[]{:S(2)}) %copy-start) | copy-done | bytes 331800
  2.9 1.0 %shard_map.77 = bf16[32,48,128]{2,1,0:T(8,128)(2,1)} custom-call(s32[1]{0:T(128)S(6)} %copy.8.order_ref, bf16[1296,128]{1,0:T(8,128)(2,1)S(1)} %copy-done, f32[2,128]{1,0:T(2,128)S(1)} %copy-done.3, f32[1,128]{1,0:T(1,128)S(1)} %bitcast.3), custom_call_target="tpu_custom_call" | custom-call | tf_op jit(solution)/shard_map/pallas_call | solution.py:179
  3.9 0.0 copy-start.1
  3.9 7.3 %all-to-all-start = ((bf16[32,48,128]{2,1,0:T(8,128)(2,1)}), bf16[32,48,128]{2,1,0:T(8,128)(2,1)S(1)}, u32[]{:S(2)}, u32[]{:S(2)}) async-start(bf16[32,48,128]{2,1,0:T(8,128)(2,1)} %shard_map.77), calls=%async_computation | async-start | bytes 786432 | tf_op jit(solution)/shard_map/all_to_all | solution.py:404
  11.2 0.7 %dynamic-slice_bitcast_fusion = f32[8,48]{1,0:T(8,128)S(1)} fusion(f32[32,8,48]{2,1,0:T(8,128)} %constant.29.clone, s32[]{:T(128)S(6)} %select_n.8), kind=kLoop, calls=%fused_computation.1 | loop fusion | bytes 3076 | tf_op jit(solution)/shard_map/broadcast_in_dim | solution.py:398
  11.9 0.1 and_or_fusion
  12.0 0.0 copy-start.4
  12.0 0.1 broadcast_select_fusion.table_ref
  12.1 12.6 %all-to-all-done.recv_ref = bf16[32,48,128]{2,1,0:T(8,128)(2,1)S(1)} async-done(((bf16[32,48,128]{2,1,0:T(8,128)(2,1)}), bf16[32,48,128]{2,1,0:T(8,128)(2,1)S(1)}, u32[]{:S(2)}, u32[]{:S(2)}) %all-to-all-start) | async-done | bytes 393248 | tf_op jit(solution)/shard_map/all_to_all | solution.py:404
  24.8 0.0 copy-done.4
  24.8 0.1 jit_solution_.3.angles_ref
  24.8 0.0 copy-done.1
  24.8 8.1 %shard_map.78 = bf16[32,48,128]{2,1,0:T(8,128)(2,1)S(1)} custom-call(s32[1]{0:T(128)S(6)} %copy.8.order_ref, bf16[32,48,128]{2,1,0:T(8,128)(2,1)S(1)} %all-to-all-done.recv_ref, bf16[1296,128]{1,0:T(8,128)(2,1)S(1)} %copy-done.1, f32[8,48,128]{2,1,0:T(8,128)S(1)} %broadcast_select_fusion.table_ref, f32[2,72,128]{2,1,0:T(8,128)S(1)} %jit_solution_.3.angles_ref), custom_call_target="tpu_custom_call" | custom-call | tf_op jit(solution)/shard_map/pallas_call | solution.py:320
  32.9 15.6 %all_to_all.10.returned_ref = bf16[32,48,128]{2,1,0:T(8,128)(2,1)S(1)} all-to-all(bf16[32,48,128]{2,1,0:T(8,128)(2,1)S(1)} %shard_map.78), channel_id=1, replica_groups=mesh['sec'=4,'dom'=8] {'sec','dom'}, dimensions={0} | all-to-all | bytes 786432 | tf_op jit(solution)/shard_map/all_to_all | solution.py:406
  48.5 0.8 %shard_map.79 = (bf16[1296,128]{1,0:T(8,128)(2,1)}, f32[2,128]{1,0:T(2,128)}) custom-call(bf16[32,48,128]{2,1,0:T(8,128)(2,1)S(1)} %all_to_all.10.returned_ref, f32[1,128]{1,0:T(1,128)S(1)} %bitcast.4), custom_call_target="tpu_custom_call" | custom-call | tf_op jit(solution)/shard_map/pallas_call | solution.py:375
  (2 shorter events, 0.0 us)
Async XLA Ops:
  1.3 0.7 %copy-start.2 = (f32[128]{0:T(128)S(1)}, f32[128]{0:T(128)}, u32[]{:S(2)}) copy-start(f32[128]{0:T(128)} %param.8) | copy-start | bytes 1540
  1.3 0.7 %copy-start.3 = (f32[2,128]{1,0:T(2,128)S(1)}, f32[2,128]{1,0:T(2,128)}, u32[]{:S(2)}) copy-start(f32[2,128]{1,0:T(2,128)} %wind_ref.1) | copy-start | bytes 3076
  2.0 1.0 %copy-start = (bf16[1296,128]{1,0:T(8,128)(2,1)S(1)}, bf16[1296,128]{1,0:T(8,128)(2,1)}, u32[]{:S(2)}) copy-start(bf16[1296,128]{1,0:T(8,128)(2,1)} %spectrum_ref.3) | copy-start | bytes 995332
  3.9 20.9 %copy-start.1 = (bf16[1296,128]{1,0:T(8,128)(2,1)S(1)}, bf16[1296,128]{1,0:T(8,128)(2,1)}, u32[]{:S(2)}) copy-start(bf16[1296,128]{1,0:T(8,128)(2,1)} %spectrum_ref.3) | copy-start | bytes 995332
  3.9 20.8 %all-to-all-start = ((bf16[32,48,128]{2,1,0:T(8,128)(2,1)}), bf16[32,48,128]{2,1,0:T(8,128)(2,1)S(1)}, u32[]{:S(2)}, u32[]{:S(2)}) async-start(bf16[32,48,128]{2,1,0:T(8,128)(2,1)} %shard_map.77), calls=%async_computation | async-start | bytes 786432 | tf_op jit(solution)/shard_map/all_to_all | solution.py:404
  12.0 12.7 %copy-start.4 = (f32[2,72]{1,0:T(2,128)S(1)}, f32[2,72]{1,0:T(2,128)}, u32[]{:S(2)}) copy-start(f32[2,72]{1,0:T(2,128)} %constant.30.clone) | copy-start | bytes 1732

commit v2 on v1

--- a/solution.py
+++ b/solution.py
@@ -26,6 +26,7 @@
 
 AXES = ("sec", "dom")
 TILE = 8
+UNROLL = 32
 GROUP_TILES = 9
 BF = jnp.bfloat16
 F32 = jnp.float32
@@ -79,7 +80,19 @@
         )
         for row, value in enumerate(values):
             table[device, row] = np.where(real, value, 0.0)
-    return table.astype(np.float32)
+    angle = np.arange(GROUP_TILES * TILE) % ND
+    angles = np.concatenate([COS[angle], SIN[angle]])
+    angles = np.broadcast_to(angles, (devices, angles.size))
+    return np.concatenate([table.reshape(devices, -1), angles], axis=1).astype(np.float32)
+
+
+def own_table(devices, me):
+    starts = table_rows(devices)[0] + [8 * layout(devices)[2]]
+    numbers = lax.dynamic_index_in_dim(jnp.asarray(device_tables(devices)), me, 0, keepdims=False)
+    row, lat = jnp.arange(numbers.shape[0])[:, None], jnp.arange(LAT)[None, :]
+    south = (row >= starts[6]) & (row < starts[7]) & (lat == 0)
+    north = (row >= starts[7]) & (row < starts[8]) & (lat == LAT - 1)
+    return jnp.where(south | north, 0.0, jnp.broadcast_to(numbers[:, None], (numbers.shape[0], LAT)))
 
 
 def split(value):
@@ -201,10 +214,10 @@
     return jnp.concatenate([main, spare, common], axis=1)
 
 
-def own_stress(spectrum_ref, angles_ref, east, north):
+def own_stress(spectrum_ref, cosine, sine, east, north):
     upper = row_ids() < TILE // 2
-    cosines = [angles_ref[0, TILE * p : TILE * (p + 1), :] for p in range(GROUP_TILES)]
-    sines = [angles_ref[1, TILE * p : TILE * (p + 1), :] for p in range(GROUP_TILES)]
+    cosines = [cosine[TILE * p : TILE * (p + 1)] for p in range(GROUP_TILES)]
+    sines = [sine[TILE * p : TILE * (p + 1)] for p in range(GROUP_TILES)]
     along = [c * east + s * north for c, s in zip(cosines, sines)]
     totals = [jnp.zeros((TILE, LAT), F32) for _ in range(GROUP_TILES)]
 
@@ -228,112 +241,127 @@
     ]
 
 
+def table_rows(devices):
+    rows = layout(devices)[2]
+    return [k * rows for k in range(8)], [8 * rows + k * GROUP_TILES * TILE for k in range(2)]
+
+
 def spread_kernel(
-    devices, section, order_ref, recv_ref, spectrum_ref, table_ref, angles_ref, out_ref,
-    field_a, field_b, wet_ref, order_vmem, order_smem, column_smem, slot_smem, sem,
+    devices, section, order_ref, recv_ref, spectrum_ref, table_ref, out_ref,
+    field_a, field_b, wet_ref, order_vmem, order_smem, slot_smem, sem,
 ):
     each, kept, rows = layout(devices)
+    starts, angle_starts = table_rows(devices)
     ids = row_ids()
     lane = lax.broadcasted_iota(jnp.int32, (TILE, LAT), 1)
-    blocks = -(-devices // LAT)
-    for block in range(blocks):
+    unit = math.gcd(devices, UNROLL)
+
+    def every(body):
+        if devices == unit:
+            for column in range(devices):
+                body(column)
+            return
+
+        def some(block, carry):
+            for k in range(unit):
+                body(block * unit + k)
+            return carry
+
+        lax.fori_loop(0, devices // unit, some, 0)
+
+    span = min(LAT, devices)
+    for block in range(devices // span):
 
         def place(s, tile, block=block):
-            here = recv_ref[block * LAT + s, kept : kept + TILE, :].astype(F32)
+            here = recv_ref[block * span + s, kept : kept + TILE, :].astype(F32)
             return jnp.where(lane == s, here, tile)
 
-        count = min(LAT, devices - block * LAT)
-        orders = lax.fori_loop(0, count, place, jnp.zeros((TILE, LAT), F32), unroll=8)
+        orders = lax.fori_loop(0, span, place, jnp.zeros((TILE, LAT), F32), unroll=min(span, UNROLL))
         order_vmem[block] = orders.astype(jnp.int32)
     copy = pltpu.make_async_copy(order_vmem, order_smem, sem)
     copy.start()
     copy.wait()
 
-    def number(s, carry):
-        column = s // section * section + order_smem[s // LAT, TILE - 1, s % LAT]
-        column_smem[s] = column
+    def number(s):
+        column = s // section * section + order_smem[s // span, TILE - 1, s % span]
         slot_smem[column] = s
-        return carry
-
-    lax.fori_loop(0, devices, number, 0, unroll=8)
+
+    every(number)
 
     def weather(column):
         tile = recv_ref[column, kept : kept + TILE, :].astype(F32)
-        east, north = tile[1:2] + tile[2:3], tile[3:4] + tile[4:5]
-        return east, north, tile[5:6] + tile[6:7]
-
-    me = lax.axis_index("sec") * section + lax.axis_index("dom")
-    stress = own_stress(spectrum_ref, angles_ref, *weather(me // section * section + order_ref[0])[:2])
-    parts = split(stress[0]) + split(stress[1])
+        return tile[1:2] + tile[2:3], tile[3:4] + tile[4:5], tile[5:6] + tile[6:7]
+
+    base = lax.axis_index("sec") * section
+    angles = [table_ref[pl.ds(start, GROUP_TILES * TILE), :] for start in angle_starts]
+    stress = own_stress(spectrum_ref, *angles, *weather(base + order_ref[0])[:2])
     column_row = jnp.full((1, LAT), order_ref[0], jnp.int32).astype(F32)
-    ending = stack_rows([None, *parts, None, None, column_row])
-
-    def renew(column, carry):
+    ending = stack_rows([None, *split(stress[0]), *split(stress[1]), None, None, column_row])
+
+    def numbers(k, first=0, count=rows):
+        return table_ref[pl.ds(starts[k] + first, count), :]
+
+    def renew(column):
         east, north, wet = weather(column)
         wet_ref[column] = jnp.broadcast_to(wet, (TILE, LAT))
         energy = recv_ref[slot_smem[column]].astype(F32)
-        push = jnp.exp(
-            jnp.maximum(0.0, table_ref[0] * east + table_ref[1] * north - table_ref[2])
-        )
-        field_a[column] = (wet * energy * push).astype(BF).astype(F32)
-        return carry
-
-    lax.fori_loop(0, devices, renew, 0, unroll=2)
-
-    def moved(source, column):
-        here = source[column]
-        west = source[jnp.where(column == 0, devices - 1, column - 1)]
-        east = source[jnp.where(column == devices - 1, 0, column + 1)]
-        total = table_ref[3] * here + table_ref[4] * west + table_ref[5] * east
-        total = total + table_ref[6] * pltpu.roll(here, 1, 1)
-        total = total + table_ref[7] * pltpu.roll(here, LAT - 1, 1)
-        return wet_ref[column, 0:1, :] * total
-
-    fields = (field_a, field_b)
-    for substep in range(SUBSTEPS - 1):
-        source, target = fields[substep % 2], fields[(substep + 1) % 2]
-
-        def step(column, carry, source=source, target=target):
-            target[column] = moved(source, column)
-            return carry
-
-        lax.fori_loop(0, devices, step, 0, unroll=2)
-    source = fields[(SUBSTEPS - 1) % 2]
-
-    def finish(column, carry):
-        total = moved(source, column)
-        last = jnp.where(ids == 0, total[kept:], ending)
-        out_ref[slot_smem[column]] = jnp.concatenate([total[:kept], last], axis=0).astype(BF)
-        return carry
-
-    lax.fori_loop(0, devices, finish, 0, unroll=2)
+        push = jnp.exp(jnp.maximum(0.0, numbers(0) * east + numbers(1) * north - numbers(2)))
+        field_a[column] = wet * energy * push
+
+    every(renew)
+
+    for substep in range(SUBSTEPS):
+        source, target = (field_a, field_b) if substep % 2 == 0 else (field_b, field_a)
+        for t in range(rows // TILE):
+            part = pl.ds(TILE * t, TILE)
+            keep, from_west, from_east, from_south, from_north = (
+                numbers(k, TILE * t, TILE) for k in range(3, 8)
+            )
+
+            def step(column):
+                if isinstance(column, int):
+                    west, east = (column - 1) % devices, (column + 1) % devices
+                else:
+                    west = jnp.where(column == 0, devices - 1, column - 1)
+                    east = jnp.where(column == devices - 1, 0, column + 1)
+                here = source[column, part, :]
+                total = keep * here + from_west * source[west, part, :]
+                total = total + from_east * source[east, part, :]
+                total = total + from_south * pltpu.roll(here, 1, 1)
+                total = total + from_north * pltpu.roll(here, LAT - 1, 1)
+                target[column, part, :] = wet_ref[column] * total
+
+            every(step)
+
+    final = field_a if SUBSTEPS % 2 == 0 else field_b
+
+    def finish(column):
+        last = jnp.where(ids == 0, final[column, kept:, :], ending)
+        whole = jnp.concatenate([final[column, :kept, :], last], axis=0)
+        out_ref[slot_smem[column]] = whole.astype(BF)
+
+    every(finish)
 
 
 def spread(devices, section, block_order, received, spectrum, table):
     each, kept, rows = layout(devices)
-    angle = np.arange(GROUP_TILES * TILE) % ND
-    angles = np.broadcast_to(
-        np.stack([COS[angle], SIN[angle]]).astype(np.float32)[:, :, None],
-        (2, GROUP_TILES * TILE, LAT),
-    )
-    blocks = -(-devices // LAT)
+    span = min(LAT, devices)
     return pl.pallas_call(
         functools.partial(spread_kernel, devices, section),
         out_shape=jax.ShapeDtypeStruct((devices, rows, LAT), BF),
-        in_specs=[smem(), vmem(), vmem(), vmem(), vmem()],
+        in_specs=[smem(), vmem(), vmem(), vmem()],
         out_specs=vmem(),
         scratch_shapes=[
             pltpu.VMEM((devices, rows, LAT), F32),
             pltpu.VMEM((devices, rows, LAT), F32),
             pltpu.VMEM((devices, TILE, LAT), F32),
-            pltpu.VMEM((blocks, TILE, LAT), jnp.int32),
-            pltpu.SMEM((blocks, TILE, LAT), jnp.int32),
-            pltpu.SMEM((devices,), jnp.int32),
+            pltpu.VMEM((devices // span, TILE, LAT), jnp.int32),
+            pltpu.SMEM((devices // span, TILE, LAT), jnp.int32),
             pltpu.SMEM((devices,), jnp.int32),
             pltpu.SemaphoreType.DMA,
         ],
         compiler_params=pltpu.CompilerParams(vmem_limit_bytes=32 << 20),
-    )(block_order, received, spectrum, table, jnp.asarray(angles))
+    )(block_order, received, spectrum, table)
 
 
 def collect(devices, section, returned_ref, wet_ref, stress_ref):
@@ -393,13 +421,7 @@
 def on_device(devices, section, spectrum, surface_wind, wet_mask, block_order):
     wet = wet_mask.reshape(1, LAT)
     each, kept, rows = layout(devices)
-    me = lax.axis_index(AXES)
-    numbers = lax.dynamic_index_in_dim(jnp.asarray(device_tables(devices)), me, 0, keepdims=False)
-    table = jnp.broadcast_to(numbers[:, :, None], (8, rows, LAT))
-    lat = jnp.arange(LAT)
-    which = jnp.arange(8)[:, None, None]
-    edge = ((which == 6) & (lat == 0)) | ((which == 7) & (lat == LAT - 1))
-    table = jnp.where(edge, 0.0, table)
+    table = own_table(devices, lax.axis_index(AXES))
     sending = packed(devices, block_order, spectrum, surface_wind, wet)
     received = lax.all_to_all(sending, AXES, split_axis=0, concat_axis=0, tiled=True)
     leaving = spread(devices, section, block_order, received, spectrum, table)

time: 49.6 us -> 44.1 us (0.89)
  Pallas kernels: 9.83 us -> 4.36 us
    pallas_call x1, Pallas kernels: 8.08 us -> 2.6 us  [spread(): pl.pallas_call(functools.partial(spread_kernel, devices, section), out_sh...]
    dynamic_slice x0 -> x1, local copies, waits for them, and re-layouts: none -> 0.75 us  [own_table(): lax.dynamic_index_in_dim(jnp.asarray(device_tables(devices)), me, 0, keep...]
    broadcast_in_dim x1 -> x0, local copies, waits for them, and re-layouts: 0.7 us -> none  [on_device(): table = jnp.broadcast_to(numbers[:, :, None], (8, rows, LAT))]
    unnamed x10 -> x8, local copies, waits for them, and re-layouts: 1.66 us -> 1.66 us
where the time goes in v2:
time: 44.1 us; the launch traced here: 43.7 us
  blocking collectives  15.6 us (35%)
  waiting for transfers between devices  12.5 us (28%)
  starting transfers between devices  7.3 us (17%)
  Pallas kernels  4.36 us (10%)
  local copies, waits for them, and re-layouts  2.41 us (5%)
  between operations  1.34 us (3%)
    all_to_all x1, blocking collectives, on_device(): lax.all_to_all(leaving, AXES, split_axis=0, concat_axis=0, tiled=True)  15.6 us
    all_to_all x1, waiting for transfers between devices, on_device(): lax.all_to_all(sending, AXES, split_axis=0, concat_axis=0, tiled=True)  12.5 us
    all_to_all x1, starting transfers between devices, on_device(): lax.all_to_all(sending, AXES, split_axis=0, concat_axis=0, tiled=True)  7.3 us
    pallas_call x1, Pallas kernels, spread(): pl.pallas_call(functools.partial(spread_kernel, devices, section), out_sh...  2.6 us
    unnamed x8, local copies, waits for them, and re-layouts  1.66 us
    pallas_call x1, Pallas kernels, packed(): pl.pallas_call(functools.partial(pack_kernel, devices), out_shape=shape,...  0.96 us
  transfers between devices with their start and end apart: 1, of which 1 were waited for; matrix products, arithmetic and copies ran while one was open for 2% of the time, Pallas kernels for 0%

profile of v2, /device:TPU:0, one launch (start us, length us, event | category | flops | bytes accessed | tf_op | source)
XLA Modules:
  0.0 43.7 jit_solution(4333552546887388454)
XLA Ops:
  1.3 0.0 copy-start.2
  1.3 0.0 copy-start.3
  1.3 0.6 %copy-done.2 = f32[128]{0:T(128)S(1)} copy-done((f32[128]{0:T(128)S(1)}, f32[128]{0:T(128)}, u32[]{:S(2)}) %copy-start.2) | copy-done | bytes 536
  1.9 0.0 copy-done.3
  2.0 0.0 copy-start
  2.0 1.0 %copy-done = bf16[1296,128]{1,0:T(8,128)(2,1)S(1)} copy-done((bf16[1296,128]{1,0:T(8,128)(2,1)S(1)}, bf16[1296,128]{1,0:T(8,128)(2,1)}, u32[]{:S(2)}) %copy-start) | copy-done | bytes 331800
  2.9 1.0 %shard_map.68 = bf16[32,48,128]{2,1,0:T(8,128)(2,1)} custom-call(s32[1]{0:T(128)S(6)} %copy.7.order_ref, bf16[1296,128]{1,0:T(8,128)(2,1)S(1)} %copy-done, f32[2,128]{1,0:T(2,128)S(1)} %copy-done.3, f32[1,128]{1,0:T(1,128)S(1)} %bitcast.1), custom_call_target="tpu_custom_call" | custom-call | tf_op jit(solution)/shard_map/pallas_call | solution.py:192
  3.9 0.0 copy-start.1
  3.9 7.3 %all-to-all-start = ((bf16[32,48,128]{2,1,0:T(8,128)(2,1)}), bf16[32,48,128]{2,1,0:T(8,128)(2,1)S(1)}, u32[]{:S(2)}, u32[]{:S(2)}) async-start(bf16[32,48,128]{2,1,0:T(8,128)(2,1)} %shard_map.68), calls=%async_computation | async-start | bytes 786432 | tf_op jit(solution)/shard_map/all_to_all | solution.py:426
  11.2 0.7 %dynamic-slice_reduce_fusion = f32[528]{0:T(1024)S(1)} fusion(f32[32,528]{1,0:T(8,128)} %constant.29.clone, s32[]{:T(128)S(6)} %select_n.8), kind=kLoop, calls=%fused_computation.7 | loop fusion | bytes 4228 | tf_op jit(solution)/shard_map/jit(dynamic_index_in_dim)/dynamic_slice | solution.py:91
  12.0 0.3 or_select_fusion.table_ref
  12.3 12.5 %all-to-all-done.recv_ref = bf16[32,48,128]{2,1,0:T(8,128)(2,1)S(1)} async-done(((bf16[32,48,128]{2,1,0:T(8,128)(2,1)}), bf16[32,48,128]{2,1,0:T(8,128)(2,1)S(1)}, u32[]{:S(2)}, u32[]{:S(2)}) %all-to-all-start) | async-done | bytes 393248 | tf_op jit(solution)/shard_map/all_to_all | solution.py:426
  24.8 0.0 copy-done.1
  24.8 2.6 %shard_map.69 = bf16[32,48,128]{2,1,0:T(8,128)(2,1)S(1)} custom-call(s32[1]{0:T(128)S(6)} %copy.7.order_ref, bf16[32,48,128]{2,1,0:T(8,128)(2,1)S(1)} %all-to-all-done.recv_ref, bf16[1296,128]{1,0:T(8,128)(2,1)S(1)} %copy-done.1, f32[528,128]{1,0:T(8,128)S(1)} %or_select_fusion.table_ref), custom_call_target="tpu_custom_call" | custom-call | tf_op jit(solution)/shard_map/pallas_call | solution.py:349
  27.4 15.6 %all_to_all.10.returned_ref = bf16[32,48,128]{2,1,0:T(8,128)(2,1)S(1)} all-to-all(bf16[32,48,128]{2,1,0:T(8,128)(2,1)S(1)} %shard_map.69), channel_id=1, replica_groups=mesh['sec'=4,'dom'=8] {'sec','dom'}, dimensions={0} | all-to-all | bytes 786432 | tf_op jit(solution)/shard_map/all_to_all | solution.py:428
  42.9 0.8 %shard_map.70 = (bf16[1296,128]{1,0:T(8,128)(2,1)}, f32[2,128]{1,0:T(2,128)}) custom-call(bf16[32,48,128]{2,1,0:T(8,128)(2,1)S(1)} %all_to_all.10.returned_ref, f32[1,128]{1,0:T(1,128)S(1)} %bitcast.2), custom_call_target="tpu_custom_call" | custom-call | tf_op jit(solution)/shard_map/pallas_call | solution.py:403
  (2 shorter events, 0.0 us)
Async XLA Ops:
  1.3 0.7 %copy-start.2 = (f32[128]{0:T(128)S(1)}, f32[128]{0:T(128)}, u32[]{:S(2)}) copy-start(f32[128]{0:T(128)} %param.7) | copy-start | bytes 1540
  1.3 0.7 %copy-start.3 = (f32[2,128]{1,0:T(2,128)S(1)}, f32[2,128]{1,0:T(2,128)}, u32[]{:S(2)}) copy-start(f32[2,128]{1,0:T(2,128)} %wind_ref.1) | copy-start | bytes 3076
  2.0 1.0 %copy-start = (bf16[1296,128]{1,0:T(8,128)(2,1)S(1)}, bf16[1296,128]{1,0:T(8,128)(2,1)}, u32[]{:S(2)}) copy-start(bf16[1296,128]{1,0:T(8,128)(2,1)} %spectrum_ref.3) | copy-start | bytes 995332
  3.9 20.9 %copy-start.1 = (bf16[1296,128]{1,0:T(8,128)(2,1)S(1)}, bf16[1296,128]{1,0:T(8,128)(2,1)}, u32[]{:S(2)}) copy-start(bf16[1296,128]{1,0:T(8,128)(2,1)} %spectrum_ref.3) | copy-start | bytes 995332
  3.9 20.8 %all-to-all-start = ((bf16[32,48,128]{2,1,0:T(8,128)(2,1)}), bf16[32,48,128]{2,1,0:T(8,128)(2,1)S(1)}, u32[]{:S(2)}, u32[]{:S(2)}) async-start(bf16[32,48,128]{2,1,0:T(8,128)(2,1)} %shard_map.68), calls=%async_computation | async-start | bytes 786432 | tf_op jit(solution)/shard_map/all_to_all | solution.py:426

commit v3 on v2

--- a/solution.py
+++ b/solution.py
@@ -27,6 +27,9 @@
 AXES = ("sec", "dom")
 TILE = 8
 UNROLL = 32
+PART = 144
+PARTS = BINS // PART
+LEAVING = 4
 GROUP_TILES = 9
 BF = jnp.bfloat16
 F32 = jnp.float32
@@ -49,6 +52,10 @@
     return pl.BlockSpec(memory_space=pltpu.SMEM)
 
 
+def anywhere():
+    return pl.BlockSpec(memory_space=pl.ANY)
+
+
 def layout(devices):
     each = BINS // devices
     rows = -(-(each + TILE) // 16) * 16
@@ -57,7 +64,7 @@
 
 def device_tables(devices):
     each, kept, rows = layout(devices)
-    table = np.zeros((devices, 8, rows), np.float64)
+    table = np.zeros((devices, rows, LAT), np.float64)
     for device in range(devices):
         bins = np.full((rows,), -1)
         bins[:each] = device * each + np.arange(each)
@@ -78,21 +85,16 @@
             np.maximum(cy, 0.0),
             np.maximum(-cy, 0.0),
         )
-        for row, value in enumerate(values):
-            table[device, row] = np.where(real, value, 0.0)
+        for lane, value in enumerate(values):
+            table[device, :, lane] = np.where(real, value, 0.0)
+    return table.astype(np.float32)
+
+
+def angle_table():
+    table = np.zeros((GROUP_TILES * TILE, LAT), np.float64)
     angle = np.arange(GROUP_TILES * TILE) % ND
-    angles = np.concatenate([COS[angle], SIN[angle]])
-    angles = np.broadcast_to(angles, (devices, angles.size))
-    return np.concatenate([table.reshape(devices, -1), angles], axis=1).astype(np.float32)
-
-
-def own_table(devices, me):
-    starts = table_rows(devices)[0] + [8 * layout(devices)[2]]
-    numbers = lax.dynamic_index_in_dim(jnp.asarray(device_tables(devices)), me, 0, keepdims=False)
-    row, lat = jnp.arange(numbers.shape[0])[:, None], jnp.arange(LAT)[None, :]
-    south = (row >= starts[6]) & (row < starts[7]) & (lat == 0)
-    north = (row >= starts[7]) & (row < starts[8]) & (lat == LAT - 1)
-    return jnp.where(south | north, 0.0, jnp.broadcast_to(numbers[:, None], (numbers.shape[0], LAT)))
+    table[:, 0], table[:, 1] = COS[angle], SIN[angle]
+    return table.astype(np.float32)
 
 
 def split(value):
@@ -117,15 +119,18 @@
     return (TILE * t) // ND, (TILE * t + TILE - 1) // ND
 
 
-def decayed_tiles(spectrum_ref):
+def decayed_tiles(spectrum_ref, arrive):
     ids = row_ids()
     upper = ids < TILE // 2
     tiles = []
-    for pair in range(BINS // 16):
-        both = spectrum_ref[16 * pair : 16 * pair + 16, :].astype(F32)
-        tiles += [both[:TILE], both[TILE:]]
     sums = [jnp.zeros((TILE, LAT), F32) for _ in range(3)]
     for group in range(NF // 2):
+        if group % 2 == 0:
+            arrive(group // 2)
+            for pair in range(GROUP_TILES):
+                first = PART * (group // 2) + 16 * pair
+                both = spectrum_ref[first : first + 16, :].astype(F32)
+                tiles += [both[:TILE], both[TILE:]]
         nine = tiles[GROUP_TILES * group : GROUP_TILES * (group + 1)]
         low = (nine[0] + nine[1]) + (nine[2] + nine[3]) + jnp.where(upper, nine[4], 0.0)
         high = (nine[5] + nine[6]) + (nine[7] + nine[8]) + jnp.where(upper, 0.0, nine[4])
@@ -143,7 +148,10 @@
         ratio = float(np.float32(WAVENUM[i])) * inverse
         factors.append(jnp.exp(-dissip_rate * (strength * (0.5 * ratio + 0.5 * ratio * ratio))))
     out = []
-    for t, tile in enumerate(tiles):
+    for t in range(BINS // TILE):
+        if t % 2 == 0:
+            both = spectrum_ref[TILE * t : TILE * t + 16, :].astype(F32)
+        tile = both[:TILE] if t % 2 == 0 else both[TILE:]
         first, last = tile_freqs(t)
         factor = factors[first]
         if last != first:
@@ -158,9 +166,43 @@
     return stack_rows([None, *east, *north, *wet, column])
 
 
-def pack_kernel(devices, order_ref, spectrum_ref, wind_ref, wet_ref, out_ref):
-    each, kept, rows = layout(devices)
-    tiles = decayed_tiles(spectrum_ref)
+def fetch(section, spectrum_hbm, wind_hbm, wet_hbm, tables_hbm, spectrum_ref, wind_ref, wet_ref, table_ref, sems):
+    me = lax.axis_index("sec") * section + lax.axis_index("dom")
+    parts = [
+        pltpu.make_async_copy(
+            spectrum_hbm.at[pl.ds(PART * k, PART), :], spectrum_ref.at[pl.ds(PART * k, PART), :], sems.at[k]
+        )
+        for k in range(PARTS)
+    ]
+    rest = [
+        pltpu.make_async_copy(source, target, sems.at[PARTS + k])
+        for k, (source, target) in enumerate(
+            ((wind_hbm, wind_ref), (wet_hbm, wet_ref), (tables_hbm.at[me], table_ref))
+        )
+    ]
+    for copy in parts + rest:
+        copy.start()
+
+    def arrive(part):
+        parts[part].wait()
+
+    def arrive_rest():
+        for copy in rest:
+            copy.wait()
+
+    return arrive, arrive_rest
+
+
+def pack_kernel(
+    devices, section, order_ref, spectrum_hbm, wind_hbm, wet_hbm, tables_hbm, out_ref, table_ref,
+    spectrum_ref, wind_ref, wet_ref, sems,
+):
+    each, kept, rows = layout(devices)
+    arrive, arrive_rest = fetch(
+        section, spectrum_hbm, wind_hbm, wet_hbm, tables_hbm, spectrum_ref, wind_ref, wet_ref, table_ref, sems
+    )
+    tiles = decayed_tiles(spectrum_ref, arrive)
+    arrive_rest()
     shared = shared_tile(wind_ref, wet_ref, order_ref[0])
     first = row_ids() == 0
     left = BINS - devices * each
@@ -175,49 +217,67 @@
         out_ref[d] = chunk.astype(BF)
 
 
-def loose_kernel(order_ref, spectrum_ref, wind_ref, wet_ref, out_ref, shared_ref):
-    tiles = decayed_tiles(spectrum_ref)
+def loose_kernel(
+    section, order_ref, spectrum_hbm, wind_hbm, wet_hbm, tables_hbm, out_ref, table_ref, shared_ref,
+    spectrum_ref, wind_ref, wet_ref, sems,
+):
+    arrive, arrive_rest = fetch(
+        section, spectrum_hbm, wind_hbm, wet_hbm, tables_hbm, spectrum_ref, wind_ref, wet_ref, table_ref, sems
+    )
+    tiles = decayed_tiles(spectrum_ref, arrive)
+    arrive_rest()
     for pair in range(BINS // 16):
         both = jnp.concatenate(tiles[2 * pair : 2 * pair + 2], axis=0)
         out_ref[16 * pair : 16 * pair + 16, :] = both.astype(BF)
     shared_ref[...] = shared_tile(wind_ref, wet_ref, order_ref[0])
 
 
-def packed(devices, block_order, spectrum, surface_wind, wet):
+def packed(devices, section, block_order, spectrum, surface_wind, wet):
     each, kept, rows = layout(devices)
     shape = jax.ShapeDtypeStruct((devices, rows, LAT), BF)
-    params = pltpu.CompilerParams(vmem_limit_bytes=24 << 20)
-    in_specs = [smem(), vmem(), vmem(), vmem()]
+    table_shape = jax.ShapeDtypeStruct((rows, LAT), F32)
+    shared = dict(
+        in_specs=[smem(), anywhere(), anywhere(), anywhere(), anywhere()],
+        scratch_shapes=[
+            pltpu.VMEM((BINS, LAT), BF),
+            pltpu.VMEM((2, LAT), F32),
+            pltpu.VMEM((1, LAT), F32),
+            pltpu.SemaphoreType.DMA((PARTS + 3,)),
+        ],
+        compiler_params=pltpu.CompilerParams(vmem_limit_bytes=24 << 20),
+    )
+    operands = (block_order, spectrum, surface_wind, wet, jnp.asarray(device_tables(devices)))
     if each == kept:
         return pl.pallas_call(
-            functools.partial(pack_kernel, devices),
-            out_shape=shape,
-            in_specs=in_specs,
-            out_specs=vmem(),
-            compiler_params=params,
-        )(block_order, spectrum, surface_wind, wet)
-    decayed, shared = pl.pallas_call(
-        loose_kernel,
+            functools.partial(pack_kernel, devices, section),
+            out_shape=(shape, table_shape),
+            out_specs=(vmem(), vmem()),
+            **shared,
+        )(*operands)
+    decayed, table, tile = pl.pallas_call(
+        functools.partial(loose_kernel, section),
         out_shape=(
             jax.ShapeDtypeStruct((BINS, LAT), BF),
+            table_shape,
             jax.ShapeDtypeStruct((TILE, LAT), F32),
         ),
-        in_specs=in_specs,
-        out_specs=(vmem(), vmem()),
-        compiler_params=params,
-    )(block_order, spectrum, surface_wind, wet)
+        out_specs=(vmem(), vmem(), vmem()),
+        **shared,
+    )(*operands)
     main = decayed[: devices * each].reshape(devices, each, LAT)
     main = jnp.pad(main, ((0, 0), (0, kept - each), (0, 0)))
     spare = decayed[devices * each :]
     spare = jnp.pad(spare, ((0, devices - spare.shape[0]), (0, 0)))[:, None]
-    common = jnp.broadcast_to(shared[1:].astype(BF)[None], (devices, TILE - 1, LAT))
-    return jnp.concatenate([main, spare, common], axis=1)
-
-
-def own_stress(spectrum_ref, cosine, sine, east, north):
+    common = jnp.broadcast_to(tile[1:].astype(BF)[None], (devices, TILE - 1, LAT))
+    return jnp.concatenate([main, spare, common], axis=1), table
+
+
+def lane_whole(rows):
+    return lax.broadcasted_iota(jnp.int32, (rows, LAT), 1)
+
+
+def own_stress(spectrum_ref, cosines, sines, east, north):
     upper = row_ids() < TILE // 2
-    cosines = [cosine[TILE * p : TILE * (p + 1)] for p in range(GROUP_TILES)]
-    sines = [sine[TILE * p : TILE * (p + 1)] for p in range(GROUP_TILES)]
     along = [c * east + s * north for c, s in zip(cosines, sines)]
     totals = [jnp.zeros((TILE, LAT), F32) for _ in range(GROUP_TILES)]
 
@@ -241,17 +301,11 @@
     ]
 
 
-def table_rows(devices):
-    rows = layout(devices)[2]
-    return [k * rows for k in range(8)], [8 * rows + k * GROUP_TILES * TILE for k in range(2)]
-
-
 def spread_kernel(
-    devices, section, order_ref, recv_ref, spectrum_ref, table_ref, out_ref,
-    field_a, field_b, wet_ref, order_vmem, order_smem, slot_smem, sem,
+    devices, section, order_ref, recv_ref, spectrum_ref, table_ref, angle_ref, out_ref,
+    field_a, field_b, wet_ref, numbers_ref, order_vmem, order_smem, slot_smem, sem,
 ):
     each, kept, rows = layout(devices)
-    starts, angle_starts = table_rows(devices)
     ids = row_ids()
     lane = lax.broadcasted_iota(jnp.int32, (TILE, LAT), 1)
     unit = math.gcd(devices, UNROLL)
@@ -280,6 +334,24 @@
         order_vmem[block] = orders.astype(jnp.int32)
     copy = pltpu.make_async_copy(order_vmem, order_smem, sem)
     copy.start()
+
+    def weather(column):
+        tile = recv_ref[column, kept : kept + TILE, :].astype(F32)
+        return tile[1:2] + tile[2:3], tile[3:4] + tile[4:5], tile[5:6] + tile[6:7]
+
+    def spread_lane(ref, t, k):
+        return jnp.broadcast_to(ref[TILE * t : TILE * (t + 1), k : k + 1], (TILE, LAT))
+
+    for t in range(rows // TILE):
+        for k in range(8):
+            numbers_ref[k, TILE * t : TILE * (t + 1), :] = spread_lane(table_ref, t, k)
+    numbers_ref[6] = jnp.where(lane_whole(rows) == 0, 0.0, numbers_ref[6])
+    numbers_ref[7] = jnp.where(lane_whole(rows) == LAT - 1, 0.0, numbers_ref[7])
+    base = lax.axis_index("sec") * section
+    angles = [[spread_lane(angle_ref, p, k) for p in range(GROUP_TILES)] for k in range(2)]
+    stress = own_stress(spectrum_ref, *angles, *weather(base + order_ref[0])[:2])
+    column_row = jnp.full((1, LAT), order_ref[0], jnp.int32).astype(F32)
+    ending = stack_rows([None, *split(stress[0]), *split(stress[1]), None, None, column_row])
     copy.wait()
 
     def number(s):
@@ -287,25 +359,12 @@
         slot_smem[column] = s
 
     every(number)
-
-    def weather(column):
-        tile = recv_ref[column, kept : kept + TILE, :].astype(F32)
-        return tile[1:2] + tile[2:3], tile[3:4] + tile[4:5], tile[5:6] + tile[6:7]
-
-    base = lax.axis_index("sec") * section
-    angles = [table_ref[pl.ds(start, GROUP_TILES * TILE), :] for start in angle_starts]
-    stress = own_stress(spectrum_ref, *angles, *weather(base + order_ref[0])[:2])
-    column_row = jnp.full((1, LAT), order_ref[0], jnp.int32).astype(F32)
-    ending = stack_rows([None, *split(stress[0]), *split(stress[1]), None, None, column_row])
-
-    def numbers(k, first=0, count=rows):
-        return table_ref[pl.ds(starts[k] + first, count), :]
 
     def renew(column):
         east, north, wet = weather(column)
         wet_ref[column] = jnp.broadcast_to(wet, (TILE, LAT))
         energy = recv_ref[slot_smem[column]].astype(F32)
-        push = jnp.exp(jnp.maximum(0.0, numbers(0) * east + numbers(1) * north - numbers(2)))
+        push = jnp.exp(jnp.maximum(0.0, numbers_ref[0] * east + numbers_ref[1] * north - numbers_ref[2]))
         field_a[column] = wet * energy * push
 
     every(renew)
@@ -315,7 +374,7 @@
         for t in range(rows // TILE):
             part = pl.ds(TILE * t, TILE)
             keep, from_west, from_east, from_south, from_north = (
-                numbers(k, TILE * t, TILE) for k in range(3, 8)
+                numbers_ref[k, part, :] for k in range(3, 8)
             )
 
             def step(column):
@@ -349,19 +408,20 @@
     return pl.pallas_call(
         functools.partial(spread_kernel, devices, section),
         out_shape=jax.ShapeDtypeStruct((devices, rows, LAT), BF),
-        in_specs=[smem(), vmem(), vmem(), vmem()],
+        in_specs=[smem(), vmem(), vmem(), vmem(), vmem()],
         out_specs=vmem(),
         scratch_shapes=[
             pltpu.VMEM((devices, rows, LAT), F32),
             pltpu.VMEM((devices, rows, LAT), F32),
             pltpu.VMEM((devices, TILE, LAT), F32),
+            pltpu.VMEM((8, rows, LAT), F32),
             pltpu.VMEM((devices // span, TILE, LAT), jnp.int32),
             pltpu.SMEM((devices // span, TILE, LAT), jnp.int32),
             pltpu.SMEM((devices,), jnp.int32),
             pltpu.SemaphoreType.DMA,
         ],
         compiler_params=pltpu.CompilerParams(vmem_limit_bytes=32 << 20),
-    )(block_order, received, spectrum, table)
+    )(block_order, received, spectrum, table, jnp.asarray(angle_table()))
 
 
 def collect(devices, section, returned_ref, wet_ref, stress_ref):
@@ -380,18 +440,31 @@
     stress_ref[1:2, :] = wet * (tile[3:4] + tile[4:5])
 
 
-def unpack_kernel(devices, section, returned_ref, wet_ref, out_ref, stress_ref):
+def unpack_kernel(devices, section, returned_ref, wet_ref, out_hbm, stress_ref, out_ref, sems):
     each, kept, rows = layout(devices)
     left = BINS - devices * each
-    for pair in range(devices // 2):
-        both = [returned_ref[2 * pair + half].astype(F32)[:each] for half in range(2)]
-        out_ref[2 * each * pair : 2 * each * (pair + 1), :] = jnp.concatenate(both, axis=0).astype(BF)
+    copies = []
+
+    def leave(first, count):
+        here = pl.ds(first, count)
+        copies.append(pltpu.make_async_copy(out_ref.at[here, :], out_hbm.at[here, :], sems.at[len(copies)]))
+        copies[-1].start()
+
     spare = []
     for tile in range(left // TILE):
         heads = [returned_ref[TILE * tile + r].astype(F32)[kept : kept + 1] for r in range(TILE)]
         spare.append(stack_rows(heads))
     out_ref[devices * each :, :] = jnp.concatenate(spare, axis=0).astype(BF)
+    leave(devices * each, left)
+    share = devices // 2 // LEAVING
+    for pair in range(devices // 2):
+        both = [returned_ref[2 * pair + half].astype(F32)[:each] for half in range(2)]
+        out_ref[2 * each * pair : 2 * each * (pair + 1), :] = jnp.concatenate(both, axis=0).astype(BF)
+        if pair % share == share - 1:
+            leave(2 * each * (pair - share + 1), 2 * each * share)
     collect(devices, section, returned_ref, wet_ref, stress_ref)
+    for copy in copies:
+        copy.wait()
 
 
 def unpacked(devices, section, returned, wet):
@@ -399,12 +472,16 @@
     left = BINS - devices * each
     stress_shape = jax.ShapeDtypeStruct((2, LAT), F32)
     params = pltpu.CompilerParams(vmem_limit_bytes=24 << 20)
-    if each == kept and devices % 2 == 0 and each % TILE == 0 and left % 16 == 0:
+    if each == kept and devices % (2 * LEAVING) == 0 and left > 0 and left % 16 == 0:
         return pl.pallas_call(
             functools.partial(unpack_kernel, devices, section),
             out_shape=(jax.ShapeDtypeStruct((BINS, LAT), BF), stress_shape),
             in_specs=[vmem(), vmem()],
-            out_specs=(vmem(), vmem()),
+            out_specs=(anywhere(), vmem()),
+            scratch_shapes=[
+                pltpu.VMEM((BINS, LAT), BF),
+                pltpu.SemaphoreType.DMA((LEAVING + 1,)),
+            ],
             compiler_params=params,
         )(returned, wet)
     stress = pl.pallas_call(
@@ -420,9 +497,7 @@
 
 def on_device(devices, section, spectrum, surface_wind, wet_mask, block_order):
     wet = wet_mask.reshape(1, LAT)
-    each, kept, rows = layout(devices)
-    table = own_table(devices, lax.axis_index(AXES))
-    sending = packed(devices, block_order, spectrum, surface_wind, wet)
+    sending, table = packed(devices, section, block_order, spectrum, surface_wind, wet)
     received = lax.all_to_all(sending, AXES, split_axis=0, concat_axis=0, tiled=True)
     leaving = spread(devices, section, block_order, received, spectrum, table)
     returned = lax.all_to_all(leaving, AXES, split_axis=0, concat_axis=0, tiled=True)

time: 44.1 us -> 45.4 us (1.029)
  blocking collectives: 15.6 us -> 36.2 us
  waiting for transfers between devices: 12.5 us -> 0 us
  starting transfers between devices: 7.3 us -> 0 us
    all_to_all x0 -> x1, blocking collectives: none -> 20.6 us  [on_device(): lax.all_to_all(sending, AXES, split_axis=0, concat_axis=0, tiled=True)]
    all_to_all x1 -> x0, waiting for transfers between devices: 12.5 us -> none  [on_device(): lax.all_to_all(sending, AXES, split_axis=0, concat_axis=0, tiled=True)]
    all_to_all x1 -> x0, starting transfers between devices: 7.3 us -> none  [on_device(): lax.all_to_all(sending, AXES, split_axis=0, concat_axis=0, tiled=True)]
    unnamed x8 -> x12, local copies, waits for them, and re-layouts: 1.66 us -> 2.8 us
    dynamic_slice x1 -> x0, local copies, waits for them, and re-layouts: 0.75 us -> none  [own_table(): lax.dynamic_index_in_dim(jnp.asarray(device_tables(devices)), me, 0, keep...]
    pallas_call x1, Pallas kernels: 0.8 us -> 1.34 us  [unpacked(): pl.pallas_call(functools.partial(unpack_kernel, devices, section), out_sh...]
  transfers between devices with their start and end apart: 1 -> 0, of which waited for: 1 -> 0; matrix products, arithmetic and copies ran while one was open for 2% -> 0% of each run, Pallas kernels for 0% -> 0%
where the time goes in v3:
time: 45.4 us; the launch traced here: 45.2 us
  blocking collectives  36.2 us (80%)
  Pallas kernels  4.81 us (11%)
  local copies, waits for them, and re-layouts  2.8 us (6%)
  between operations  1.33 us (3%)
    all_to_all x1, blocking collectives, on_device(): lax.all_to_all(sending, AXES, split_axis=0, concat_axis=0, tiled=True)  20.6 us
    all_to_all x1, blocking collectives, on_device(): lax.all_to_all(leaving, AXES, split_axis=0, concat_axis=0, tiled=True)  15.6 us
    unnamed x12, local copies, waits for them, and re-layouts  2.8 us
    pallas_call x1, Pallas kernels, spread(): pl.pallas_call(functools.partial(spread_kernel, devices, section), out_sh...  2.68 us
    pallas_call x1, Pallas kernels, unpacked(): pl.pallas_call(functools.partial(unpack_kernel, devices, section), out_sh...  1.34 us

profile of v3, /device:TPU:0, one launch (start us, length us, event | category | flops | bytes accessed | tf_op | source)
XLA Modules:
  0.0 45.2 jit_solution(14780180993001886265)
XLA Ops:
  1.3 0.0 copy-start.4
  1.3 0.0 copy-start.5
  1.3 0.6 %copy-done.4 = f32[128]{0:T(128)S(1)} copy-done((f32[128]{0:T(128)S(1)}, f32[128]{0:T(128)}, u32[]{:S(2)}) %copy-start.4) | copy-done | bytes 536
  1.9 0.0 copy-done.5
  2.0 0.0 copy-start
  2.0 1.0 %copy-done = bf16[1296,128]{1,0:T(8,128)(2,1)S(1)} copy-done((bf16[1296,128]{1,0:T(8,128)(2,1)S(1)}, bf16[1296,128]{1,0:T(8,128)(2,1)}, u32[]{:S(2)}) %copy-start) | copy-done | bytes 331800
  2.9 0.0 copy-start.2
  3.0 1.1 %copy-done.2 = f32[32,48,128]{2,1,0:T(8,128)S(1)} copy-done((f32[32,48,128]{2,1,0:T(8,128)S(1)}, f32[32,48,128]{2,1,0:T(8,128)}, u32[]{:S(2)}) %copy-start.2) | copy-done | bytes 786456
  4.1 0.8 %shard_map.77 = (bf16[32,48,128]{2,1,0:T(8,128)(2,1)S(1)}, f32[48,128]{1,0:T(8,128)S(1)}) custom-call(s32[1]{0:T(128)S(6)} %copy.8.order_ref, bf16[1296,128]{1,0:T(8,128)(2,1)S(1)} %copy-done, f32[2,128]{1,0:T(2,128)S(1)} %copy-done.5, f32[1,128]{1,0:T(1,128)S(1)} %bitcast.1, f32[32,48,128]{2,1,0:T(8,128)S(1)} %copy-done.2), custom_call_target="tpu_custom_call" | custom-call | tf_op jit(solution)/shard_map/pallas_call | solution.py:251
  4.9 0.0 copy-start.1
  4.9 0.0 copy-start.3
  4.9 20.6 %all_to_all.10.recv_ref = bf16[32,48,128]{2,1,0:T(8,128)(2,1)S(1)} all-to-all(bf16[32,48,128]{2,1,0:T(8,128)(2,1)S(1)} %get-tuple-element.4), channel_id=1, replica_groups=mesh['sec'=4,'dom'=8] {'sec','dom'}, dimensions={0} | all-to-all | bytes 786432 | tf_op jit(solution)/shard_map/all_to_all | solution.py:501
  25.5 0.0 copy-done.1
  25.6 0.0 copy-done.3
  25.6 2.7 %shard_map.78 = bf16[32,48,128]{2,1,0:T(8,128)(2,1)S(1)} custom-call(s32[1]{0:T(128)S(6)} %copy.8.order_ref, bf16[32,48,128]{2,1,0:T(8,128)(2,1)S(1)} %all_to_all.10.recv_ref, bf16[1296,128]{1,0:T(8,128)(2,1)S(1)} %copy-done.1, f32[48,128]{1,0:T(8,128)S(1)} %get-tuple-element.5.table_ref, f32[72,128]{1,0:T(8,128)S(1)} %copy-done.3), custom_call_target="tpu_custom_call" | custom-call | tf_op jit(solution)/shard_map/pallas_call | solution.py:408
  28.2 15.6 %all_to_all.11.returned_ref = bf16[32,48,128]{2,1,0:T(8,128)(2,1)S(1)} all-to-all(bf16[32,48,128]{2,1,0:T(8,128)(2,1)S(1)} %shard_map.78), channel_id=1, replica_groups=mesh['sec'=4,'dom'=8] {'sec','dom'}, dimensions={0} | all-to-all | bytes 786432 | tf_op jit(solution)/shard_map/all_to_all | solution.py:503
  43.8 1.3 %shard_map.79 = (bf16[1296,128]{1,0:T(8,128)(2,1)}, f32[2,128]{1,0:T(2,128)}) custom-call(bf16[32,48,128]{2,1,0:T(8,128)(2,1)S(1)} %all_to_all.11.returned_ref, f32[1,128]{1,0:T(1,128)S(1)} %bitcast.2), custom_call_target="tpu_custom_call" | custom-call | tf_op jit(solution)/shard_map/pallas_call | solution.py:476
Async XLA Ops:
  1.3 0.7 %copy-start.4 = (f32[128]{0:T(128)S(1)}, f32[128]{0:T(128)}, u32[]{:S(2)}) copy-start(f32[128]{0:T(128)} %param.8) | copy-start | bytes 1540
  1.3 0.7 %copy-start.5 = (f32[2,128]{1,0:T(2,128)S(1)}, f32[2,128]{1,0:T(2,128)}, u32[]{:S(2)}) copy-start(f32[2,128]{1,0:T(2,128)} %wind_hbm.1) | copy-start | bytes 3076
  2.0 1.0 %copy-start = (bf16[1296,128]{1,0:T(8,128)(2,1)S(1)}, bf16[1296,128]{1,0:T(8,128)(2,1)}, u32[]{:S(2)}) copy-start(bf16[1296,128]{1,0:T(8,128)(2,1)} %spectrum_ref.1) | copy-start | bytes 995332
  2.9 1.1 %copy-start.2 = (f32[32,48,128]{2,1,0:T(8,128)S(1)}, f32[32,48,128]{2,1,0:T(8,128)}, u32[]{:S(2)}) copy-start(f32[32,48,128]{2,1,0:T(8,128)} %constant.4.clone.tables_hbm) | copy-start | bytes 2359300
  4.9 20.7 %copy-start.1 = (bf16[1296,128]{1,0:T(8,128)(2,1)S(1)}, bf16[1296,128]{1,0:T(8,128)(2,1)}, u32[]{:S(2)}) copy-start(bf16[1296,128]{1,0:T(8,128)(2,1)} %spectrum_ref.1) | copy-start | bytes 995332
  4.9 20.7 %copy-start.3 = (f32[72,128]{1,0:T(8,128)S(1)}, f32[72,128]{1,0:T(8,128)}, u32[]{:S(2)}) copy-start(f32[72,128]{1,0:T(8,128)} %constant.5.clone.angle_ref) | copy-start | bytes 110596

commit v4 on v3

--- a/solution.py
+++ b/solution.py
@@ -27,9 +27,9 @@
 AXES = ("sec", "dom")
 TILE = 8
 UNROLL = 32
+BATCH = 8
 PART = 144
 PARTS = BINS // PART
-LEAVING = 4
 GROUP_TILES = 9
 BF = jnp.bfloat16
 F32 = jnp.float32
@@ -40,8 +40,7 @@
 SPEED = gravity / SIGMA
 AREA = 0.1 * SIGMA * (2.0 * math.pi / ND)
 THETA = 2.0 * math.pi * np.arange(ND, dtype=np.float64) / ND
-COS = np.cos(THETA)
-SIN = np.sin(THETA)
+COS, SIN = (np.where(np.abs(wave) < 1e-9, 0.0, wave) for wave in (np.cos(THETA), np.sin(THETA)))
 
 
 def vmem():
@@ -52,8 +51,8 @@
     return pl.BlockSpec(memory_space=pltpu.SMEM)
 
 
-def anywhere():
-    return pl.BlockSpec(memory_space=pl.ANY)
+def hbm():
+    return pl.BlockSpec(memory_space=pltpu.HBM)
 
 
 def layout(devices):
@@ -62,12 +61,40 @@
     return each, rows - TILE, rows
 
 
+def tile_slots(devices):
+    each, kept, rows = layout(devices)
+    if each != kept:
+        return None, 0
+    count, half = each // TILE, devices // 2
+    ways = [[], [], []]
+    for t in range(devices * count):
+        wave = SIN[(TILE * t + np.arange(TILE)) % ND]
+        ways[0 if (wave >= 0).all() else 1 if (wave <= 0).all() else 2].append(t)
+    sure = min(len(ways[0]) // half, len(ways[1]) // half, count)
+    rest = sorted(ways[0][sure * half :] + ways[1][sure * half :] + ways[2])
+    slots = []
+    for d in range(devices):
+        way, place = ways[d // half], d % half
+        mixed = rest[(count - sure) * d : (count - sure) * (d + 1)]
+        slots.append(way[sure * place : sure * (place + 1)] + mixed)
+    return slots, sure
+
+
+def spare_way(devices):
+    wave = SIN[np.arange(BINS // devices * devices, BINS) % ND]
+    return 1 if (wave >= 0).all() else -1 if (wave <= 0).all() else 0
+
+
 def device_tables(devices):
     each, kept, rows = layout(devices)
+    slots = tile_slots(devices)[0]
     table = np.zeros((devices, rows, LAT), np.float64)
     for device in range(devices):
         bins = np.full((rows,), -1)
-        bins[:each] = device * each + np.arange(each)
+        if slots is None:
+            bins[:each] = device * each + np.arange(each)
+        else:
+            bins[:each] = (TILE * np.array(slots[device])[:, None] + np.arange(TILE)).reshape(-1)
         if devices * each + device < BINS:
             bins[kept] = devices * each + device
         real = bins >= 0
@@ -147,17 +174,15 @@
     for i in range(NF):
         ratio = float(np.float32(WAVENUM[i])) * inverse
         factors.append(jnp.exp(-dissip_rate * (strength * (0.5 * ratio + 0.5 * ratio * ratio))))
-    out = []
-    for t in range(BINS // TILE):
-        if t % 2 == 0:
-            both = spectrum_ref[TILE * t : TILE * t + 16, :].astype(F32)
-        tile = both[:TILE] if t % 2 == 0 else both[TILE:]
+
+    def decayed(t):
         first, last = tile_freqs(t)
         factor = factors[first]
         if last != first:
             factor = jnp.where(upper, factor, factors[last])
-        out.append(tile * factor)
-    return out
+        return spectrum_ref[TILE * t : TILE * (t + 1), :].astype(F32) * factor
+
+    return decayed
 
 
 def shared_tile(wind_ref, wet_ref, order):
@@ -201,19 +226,19 @@
     arrive, arrive_rest = fetch(
         section, spectrum_hbm, wind_hbm, wet_hbm, tables_hbm, spectrum_ref, wind_ref, wet_ref, table_ref, sems
     )
-    tiles = decayed_tiles(spectrum_ref, arrive)
+    decayed = decayed_tiles(spectrum_ref, arrive)
     arrive_rest()
     shared = shared_tile(wind_ref, wet_ref, order_ref[0])
     first = row_ids() == 0
     left = BINS - devices * each
-    per = each // TILE
+    slots = tile_slots(devices)[0]
+    spares = [decayed(t) for t in range(devices * each // TILE, BINS // TILE)]
     for d in range(devices):
         last = shared
         if d < left:
-            spare = tiles[per * devices + d // TILE]
-            row = spare[d % TILE : d % TILE + 1]
+            row = spares[d // TILE][d % TILE : d % TILE + 1]
             last = jnp.where(first, jnp.broadcast_to(row, (TILE, LAT)), shared)
-        chunk = jnp.concatenate(tiles[per * d : per * (d + 1)] + [last], axis=0)
+        chunk = jnp.concatenate([decayed(t) for t in slots[d]] + [last], axis=0)
         out_ref[d] = chunk.astype(BF)
 
 
@@ -224,10 +249,10 @@
     arrive, arrive_rest = fetch(
         section, spectrum_hbm, wind_hbm, wet_hbm, tables_hbm, spectrum_ref, wind_ref, wet_ref, table_ref, sems
     )
-    tiles = decayed_tiles(spectrum_ref, arrive)
+    decayed = decayed_tiles(spectrum_ref, arrive)
     arrive_rest()
     for pair in range(BINS // 16):
-        both = jnp.concatenate(tiles[2 * pair : 2 * pair + 2], axis=0)
+        both = jnp.concatenate([decayed(2 * pair), decayed(2 * pair + 1)], axis=0)
         out_ref[16 * pair : 16 * pair + 16, :] = both.astype(BF)
     shared_ref[...] = shared_tile(wind_ref, wet_ref, order_ref[0])
 
@@ -237,14 +262,14 @@
     shape = jax.ShapeDtypeStruct((devices, rows, LAT), BF)
     table_shape = jax.ShapeDtypeStruct((rows, LAT), F32)
     shared = dict(
-        in_specs=[smem(), anywhere(), anywhere(), anywhere(), anywhere()],
+        in_specs=[smem(), hbm(), hbm(), hbm(), hbm()],
         scratch_shapes=[
             pltpu.VMEM((BINS, LAT), BF),
             pltpu.VMEM((2, LAT), F32),
             pltpu.VMEM((1, LAT), F32),
             pltpu.SemaphoreType.DMA((PARTS + 3,)),
         ],
-        compiler_params=pltpu.CompilerParams(vmem_limit_bytes=24 << 20),
+        compiler_params=pltpu.CompilerParams(vmem_limit_bytes=60 << 20),
     )
     operands = (block_order, spectrum, surface_wind, wet, jnp.asarray(device_tables(devices)))
     if each == kept:
@@ -303,22 +328,22 @@
 
 def spread_kernel(
     devices, section, order_ref, recv_ref, spectrum_ref, table_ref, angle_ref, out_ref,
-    field_a, field_b, wet_ref, numbers_ref, order_vmem, order_smem, slot_smem, sem,
+    field_a, field_b, wet_ref, numbers_ref, slot_smem,
 ):
     each, kept, rows = layout(devices)
     ids = row_ids()
     lane = lax.broadcasted_iota(jnp.int32, (TILE, LAT), 1)
     unit = math.gcd(devices, UNROLL)
 
-    def every(body):
+    def every(body, batch=1):
         if devices == unit:
-            for column in range(devices):
-                body(column)
+            for k in range(0, unit, batch):
+                body(*range(k, k + batch))
             return
 
         def some(block, carry):
-            for k in range(unit):
-                body(block * unit + k)
+            for k in range(0, unit, batch):
+                body(*(block * unit + k + n for n in range(batch)))
             return carry
 
         lax.fori_loop(0, devices // unit, some, 0)
@@ -331,9 +356,9 @@
             return jnp.where(lane == s, here, tile)
 
         orders = lax.fori_loop(0, span, place, jnp.zeros((TILE, LAT), F32), unroll=min(span, UNROLL))
-        order_vmem[block] = orders.astype(jnp.int32)
-    copy = pltpu.make_async_copy(order_vmem, order_smem, sem)
-    copy.start()
+        last = orders[TILE - 1 :].astype(jnp.int32)
+        for s in range(span):
+            slot_smem[(block * span + s) // section * section + last[0, s]] = block * span + s
 
     def weather(column):
         tile = recv_ref[column, kept : kept + TILE, :].astype(F32)
@@ -348,18 +373,11 @@
     numbers_ref[6] = jnp.where(lane_whole(rows) == 0, 0.0, numbers_ref[6])
     numbers_ref[7] = jnp.where(lane_whole(rows) == LAT - 1, 0.0, numbers_ref[7])
     base = lax.axis_index("sec") * section
+    me = base + lax.axis_index("dom")
     angles = [[spread_lane(angle_ref, p, k) for p in range(GROUP_TILES)] for k in range(2)]
     stress = own_stress(spectrum_ref, *angles, *weather(base + order_ref[0])[:2])
     column_row = jnp.full((1, LAT), order_ref[0], jnp.int32).astype(F32)
     ending = stack_rows([None, *split(stress[0]), *split(stress[1]), None, None, column_row])
-    copy.wait()
-
-    def number(s):
-        column = s // section * section + order_smem[s // span, TILE - 1, s % span]
-        slot_smem[column] = s
-
-    every(number)
-
     def renew(column):
         east, north, wet = weather(column)
         wet_ref[column] = jnp.broadcast_to(wet, (TILE, LAT))
@@ -369,37 +387,61 @@
 
     every(renew)
 
-    for substep in range(SUBSTEPS):
+    def around(column):
+        if isinstance(column, int):
+            return (column - 1) % devices, (column + 1) % devices
+        return jnp.where(column == 0, devices - 1, column - 1), jnp.where(column == devices - 1, 0, column + 1)
+
+    sure = tile_slots(devices)[1]
+    northward = me < devices // 2
+
+    def mover(source, t):
+        part = pl.ds(TILE * t, TILE)
+        keep, from_west, from_east, from_south, from_north = (numbers_ref[k, part, :] for k in range(3, 8))
+        westerly, southerly = from_west > 0.0, from_south > 0.0
+        from_x, from_y = from_west + from_east, from_south + from_north
+        way = spare_way(devices) if TILE * t == kept else 0
+
+        def shifted(here):
+            if t < sure:
+                return pltpu.roll(here, jnp.where(northward, 1, LAT - 1), 1)
+            if way:
+                return pltpu.roll(here, way % LAT, 1)
+            return jnp.where(southerly, pltpu.roll(here, 1, 1), pltpu.roll(here, LAT - 1, 1))
+
+        def moved(column):
+            west, east = around(column)
+            here = source[column, part, :]
+            total = keep * here + from_x * jnp.where(westerly, source[west, part, :], source[east, part, :])
+            return wet_ref[column] * (total + from_y * shifted(here))
+
+        return moved
+
+    for substep in range(SUBSTEPS - 1):
         source, target = (field_a, field_b) if substep % 2 == 0 else (field_b, field_a)
         for t in range(rows // TILE):
-            part = pl.ds(TILE * t, TILE)
-            keep, from_west, from_east, from_south, from_north = (
-                numbers_ref[k, part, :] for k in range(3, 8)
-            )
+            moved = mover(source, t)
 
             def step(column):
-                if isinstance(column, int):
-                    west, east = (column - 1) % devices, (column + 1) % devices
-                else:
-                    west = jnp.where(column == 0, devices - 1, column - 1)
-                    east = jnp.where(column == devices - 1, 0, column + 1)
-                here = source[column, part, :]
-                total = keep * here + from_west * source[west, part, :]
-                total = total + from_east * source[east, part, :]
-                total = total + from_south * pltpu.roll(here, 1, 1)
-                total = total + from_north * pltpu.roll(here, LAT - 1, 1)
-                target[column, part, :] = wet_ref[column] * total
+                target[column, TILE * t : TILE * (t + 1), :] = moved(column)
 
             every(step)
 
-    final = field_a if SUBSTEPS % 2 == 0 else field_b
-
-    def finish(column):
-        last = jnp.where(ids == 0, final[column, kept:, :], ending)
-        whole = jnp.concatenate([final[column, :kept, :], last], axis=0)
-        out_ref[slot_smem[column]] = whole.astype(BF)
-
-    every(finish)
+    source = field_a if (SUBSTEPS - 1) % 2 == 0 else field_b
+    for t in range(0, rows // TILE, 2):
+        upper_tile, lower_tile = mover(source, t), mover(source, t + 1)
+
+        def finish(*columns):
+            made = []
+            for column in columns:
+                upper, lower = upper_tile(column), lower_tile(column)
+                if TILE * (t + 1) == kept:
+                    lower = jnp.where(ids == 0, lower, ending)
+                made.append(jnp.concatenate([upper, lower], axis=0).astype(BF))
+            for column, value in zip(columns, made):
+                out_ref[slot_smem[column], TILE * t : TILE * (t + 2), :] = value
+
+        every(finish, min(BATCH, unit))
 
 
 def spread(devices, section, block_order, received, spectrum, table):
@@ -415,10 +457,7 @@
             pltpu.VMEM((devices, rows, LAT), F32),
             pltpu.VMEM((devices, TILE, LAT), F32),
             pltpu.VMEM((8, rows, LAT), F32),
-            pltpu.VMEM((devices // span, TILE, LAT), jnp.int32),
-            pltpu.SMEM((devices // span, TILE, LAT), jnp.int32),
             pltpu.SMEM((devices,), jnp.int32),
-            pltpu.SemaphoreType.DMA,
         ],
         compiler_params=pltpu.CompilerParams(vmem_limit_bytes=32 << 20),
     )(block_order, received, spectrum, table, jnp.asarray(angle_table()))
@@ -440,31 +479,20 @@
     stress_ref[1:2, :] = wet * (tile[3:4] + tile[4:5])
 
 
-def unpack_kernel(devices, section, returned_ref, wet_ref, out_hbm, stress_ref, out_ref, sems):
+def unpack_kernel(devices, section, returned_ref, wet_ref, out_ref, stress_ref):
     each, kept, rows = layout(devices)
     left = BINS - devices * each
-    copies = []
-
-    def leave(first, count):
-        here = pl.ds(first, count)
-        copies.append(pltpu.make_async_copy(out_ref.at[here, :], out_hbm.at[here, :], sems.at[len(copies)]))
-        copies[-1].start()
-
+    home = {t: (d, k) for d, tiles in enumerate(tile_slots(devices)[0]) for k, t in enumerate(tiles)}
+    for pair in range(devices * each // 16):
+        for t in (2 * pair, 2 * pair + 1):
+            d, k = home[t]
+            out_ref[TILE * t : TILE * (t + 1), :] = returned_ref[d, TILE * k : TILE * (k + 1), :]
     spare = []
     for tile in range(left // TILE):
         heads = [returned_ref[TILE * tile + r].astype(F32)[kept : kept + 1] for r in range(TILE)]
         spare.append(stack_rows(heads))
     out_ref[devices * each :, :] = jnp.concatenate(spare, axis=0).astype(BF)
-    leave(devices * each, left)
-    share = devices // 2 // LEAVING
-    for pair in range(devices // 2):
-        both = [returned_ref[2 * pair + half].astype(F32)[:each] for half in range(2)]
-        out_ref[2 * each * pair : 2 * each * (pair + 1), :] = jnp.concatenate(both, axis=0).astype(BF)
-        if pair % share == share - 1:
-            leave(2 * each * (pair - share + 1), 2 * each * share)
     collect(devices, section, returned_ref, wet_ref, stress_ref)
-    for copy in copies:
-        copy.wait()
 
 
 def unpacked(devices, section, returned, wet):
@@ -472,16 +500,12 @@
     left = BINS - devices * each
     stress_shape = jax.ShapeDtypeStruct((2, LAT), F32)
     params = pltpu.CompilerParams(vmem_limit_bytes=24 << 20)
-    if each == kept and devices % (2 * LEAVING) == 0 and left > 0 and left % 16 == 0:
+    if each == kept and devices % 2 == 0 and each % TILE == 0 and left % 16 == 0:
         return pl.pallas_call(
             functools.partial(unpack_kernel, devices, section),
             out_shape=(jax.ShapeDtypeStruct((BINS, LAT), BF), stress_shape),
             in_specs=[vmem(), vmem()],
-            out_specs=(anywhere(), vmem()),
-            scratch_shapes=[
-                pltpu.VMEM((BINS, LAT), BF),
-                pltpu.SemaphoreType.DMA((LEAVING + 1,)),
-            ],
+            out_specs=(vmem(), vmem()),
             compiler_params=params,
         )(returned, wet)
     stress = pl.pallas_call(

time: 45.4 us -> 42.4 us (0.934)
  local copies, waits for them, and re-layouts: 2.8 us -> 0.03 us
  Pallas kernels: 4.81 us -> 4.35 us
    unnamed x12 -> x8, local copies, waits for them, and re-layouts: 2.8 us -> 0.03 us
    pallas_call x1, Pallas kernels: 0.79 us -> 1.92 us  [packed(): pl.pallas_call(functools.partial(pack_kernel, devices, section), out_shap...]
    pallas_call x1, Pallas kernels: 2.68 us -> 1.65 us  [spread(): pl.pallas_call(functools.partial(spread_kernel, devices, section), out_sh...]
    pallas_call x1, Pallas kernels: 1.34 us -> 0.78 us  [unpacked(): pl.pallas_call(functools.partial(unpack_kernel, devices, section), out_sh...]
where the time goes in v4:
time: 42.4 us; the launch traced here: 42.1 us
  blocking collectives  36.4 us (86%)
  Pallas kernels  4.35 us (10%)
  between operations  1.33 us (3%)
    all_to_all x1, blocking collectives, on_device(): lax.all_to_all(sending, AXES, split_axis=0, concat_axis=0, tiled=True)  20.9 us
    all_to_all x1, blocking collectives, on_device(): lax.all_to_all(leaving, AXES, split_axis=0, concat_axis=0, tiled=True)  15.6 us
    pallas_call x1, Pallas kernels, packed(): pl.pallas_call(functools.partial(pack_kernel, devices, section), out_shap...  1.92 us
    pallas_call x1, Pallas kernels, spread(): pl.pallas_call(functools.partial(spread_kernel, devices, section), out_sh...  1.65 us

profile of v4, /device:TPU:0, one launch (start us, length us, event | category | flops | bytes accessed | tf_op | source)
XLA Modules:
  0.0 42.1 jit_solution(17444230078698377831)
XLA Ops:
  1.3 1.9 %shard_map.77 = (bf16[32,48,128]{2,1,0:T(8,128)(2,1)}, f32[48,128]{1,0:T(8,128)}) custom-call(s32[1]{0:T(128)S(6)} %copy.8.order_ref, bf16[1296,128]{1,0:T(8,128)(2,1)} %spectrum_ref.1, f32[2,128]{1,0:T(2,128)} %wind_hbm.1, f32[1,128]{1,0:T(1,128)} %bitcast.1, f32[32,48,128]{2,1,0:T(8,128)} %constant.4.clone.tables_hbm), custom_call_target="tpu_custom_call" | custom-call | tf_op jit(solution)/shard_map/pallas_call | solution.py:276
  3.2 0.0 copy-start
  3.2 0.0 copy-start.1
  3.2 0.0 copy-start.2
  3.2 20.9 %all_to_all.10.recv_ref = bf16[32,48,128]{2,1,0:T(8,128)(2,1)S(1)} all-to-all(bf16[32,48,128]{2,1,0:T(8,128)(2,1)} %get-tuple-element.4), channel_id=1, replica_groups=mesh['sec'=4,'dom'=8] {'sec','dom'}, dimensions={0} | all-to-all | bytes 786432 | tf_op jit(solution)/shard_map/all_to_all | solution.py:525
  24.1 0.0 copy-done
  24.1 0.0 copy-done.1
  24.1 0.0 copy-done.2
  24.1 1.6 %shard_map.78 = bf16[32,48,128]{2,1,0:T(8,128)(2,1)S(1)} custom-call(s32[1]{0:T(128)S(6)} %copy.8.order_ref, bf16[32,48,128]{2,1,0:T(8,128)(2,1)S(1)} %all_to_all.10.recv_ref, bf16[1296,128]{1,0:T(8,128)(2,1)S(1)} %copy-done, f32[48,128]{1,0:T(8,128)S(1)} %copy-done.2, f32[72,128]{1,0:T(8,128)S(1)} %copy-done.1), custom_call_target="tpu_custom_call" | custom-call | tf_op jit(solution)/shard_map/pallas_call | solution.py:450
  25.8 0.0 copy-start.3
  25.8 15.6 %all_to_all.11.returned_ref = bf16[32,48,128]{2,1,0:T(8,128)(2,1)S(1)} all-to-all(bf16[32,48,128]{2,1,0:T(8,128)(2,1)S(1)} %shard_map.78), channel_id=1, replica_groups=mesh['sec'=4,'dom'=8] {'sec','dom'}, dimensions={0} | all-to-all | bytes 786432 | tf_op jit(solution)/shard_map/all_to_all | solution.py:527
  41.3 0.0 copy-done.3
  41.4 0.8 %shard_map.79 = (bf16[1296,128]{1,0:T(8,128)(2,1)}, f32[2,128]{1,0:T(2,128)}) custom-call(bf16[32,48,128]{2,1,0:T(8,128)(2,1)S(1)} %all_to_all.11.returned_ref, f32[1,128]{1,0:T(1,128)S(1)} %bitcast.2), custom_call_target="tpu_custom_call" | custom-call | tf_op jit(solution)/shard_map/pallas_call | solution.py:504
Async XLA Ops:
  3.2 20.9 %copy-start = (bf16[1296,128]{1,0:T(8,128)(2,1)S(1)}, bf16[1296,128]{1,0:T(8,128)(2,1)}, u32[]{:S(2)}) copy-start(bf16[1296,128]{1,0:T(8,128)(2,1)} %spectrum_ref.1) | copy-start | bytes 995332
  3.2 20.9 %copy-start.1 = (f32[72,128]{1,0:T(8,128)S(1)}, f32[72,128]{1,0:T(8,128)}, u32[]{:S(2)}) copy-start(f32[72,128]{1,0:T(8,128)} %constant.5.clone.angle_ref) | copy-start | bytes 110596
  3.2 20.9 %copy-start.2 = (f32[48,128]{1,0:T(8,128)S(1)}, f32[48,128]{1,0:T(8,128)}, u32[]{:S(2)}) copy-start(f32[48,128]{1,0:T(8,128)} %get-tuple-element.5.table_ref) | copy-start | bytes 73732
  25.8 15.6 %copy-start.3 = (f32[128]{0:T(128)S(1)}, f32[128]{0:T(128)}, u32[]{:S(2)}) copy-start(f32[128]{0:T(128)} %param.8) | copy-start | bytes 1540

commit v5 on v4

--- a/solution.py
+++ b/solution.py
@@ -26,6 +26,7 @@
 
 AXES = ("sec", "dom")
 TILE = 8
+QUAD = 4
 UNROLL = 32
 BATCH = 8
 PART = 144
@@ -377,7 +378,7 @@
     angles = [[spread_lane(angle_ref, p, k) for p in range(GROUP_TILES)] for k in range(2)]
     stress = own_stress(spectrum_ref, *angles, *weather(base + order_ref[0])[:2])
     column_row = jnp.full((1, LAT), order_ref[0], jnp.int32).astype(F32)
-    ending = stack_rows([None, *split(stress[0]), *split(stress[1]), None, None, column_row])
+    ending = stack_rows([None, stress[0], stress[1], column_row])
     def renew(column):
         east, north, wet = weather(column)
         wet_ref[column] = jnp.broadcast_to(wet, (TILE, LAT))
@@ -427,6 +428,7 @@
 
             every(step)
 
+    back = (kept + QUAD) // QUAD
     source = field_a if (SUBSTEPS - 1) % 2 == 0 else field_b
     for t in range(0, rows // TILE, 2):
         upper_tile, lower_tile = mover(source, t), mover(source, t + 1)
@@ -437,9 +439,11 @@
                 upper, lower = upper_tile(column), lower_tile(column)
                 if TILE * (t + 1) == kept:
                     lower = jnp.where(ids == 0, lower, ending)
-                made.append(jnp.concatenate([upper, lower], axis=0).astype(BF))
+                made.append(jnp.concatenate([upper, lower], axis=0))
             for column, value in zip(columns, made):
-                out_ref[slot_smem[column], TILE * t : TILE * (t + 2), :] = value
+                for piece in range(min(4, back - 4 * (t // 2))):
+                    quarter = value[QUAD * piece : QUAD * (piece + 1)].astype(BF)
+                    out_ref[slot_smem[column], 4 * (t // 2) + piece] = quarter
 
         every(finish, min(BATCH, unit))
 
@@ -449,7 +453,7 @@
     span = min(LAT, devices)
     return pl.pallas_call(
         functools.partial(spread_kernel, devices, section),
-        out_shape=jax.ShapeDtypeStruct((devices, rows, LAT), BF),
+        out_shape=jax.ShapeDtypeStruct((devices, (kept + QUAD) // QUAD, QUAD, LAT), BF),
         in_specs=[smem(), vmem(), vmem(), vmem(), vmem()],
         out_specs=vmem(),
         scratch_shapes=[
@@ -469,14 +473,12 @@
     rank = lax.axis_index("dom").astype(F32)
 
     def pick(s, total):
-        tile = returned_ref[base + s, kept : kept + TILE, :].astype(F32)
-        mine = jnp.broadcast_to(tile[TILE - 1 : TILE] == rank, (TILE, LAT))
+        tile = returned_ref[base + s, kept // QUAD].astype(F32)
+        mine = jnp.broadcast_to(tile[QUAD - 1 : QUAD] == rank, (QUAD, LAT))
         return jnp.where(mine, tile, total)
 
-    tile = lax.fori_loop(0, section, pick, jnp.zeros((TILE, LAT), F32), unroll=8)
-    wet = wet_ref[0:1, :]
-    stress_ref[0:1, :] = wet * (tile[1:2] + tile[2:3])
-    stress_ref[1:2, :] = wet * (tile[3:4] + tile[4:5])
+    tile = lax.fori_loop(0, section, pick, jnp.zeros((QUAD, LAT), F32), unroll=8)
+    stress_ref[...] = wet_ref[0:1, :] * tile[1:3]
 
 
 def unpack_kernel(devices, section, returned_ref, wet_ref, out_ref, stress_ref):
@@ -484,12 +486,13 @@
     left = BINS - devices * each
     home = {t: (d, k) for d, tiles in enumerate(tile_slots(devices)[0]) for k, t in enumerate(tiles)}
     for pair in range(devices * each // 16):
-        for t in (2 * pair, 2 * pair + 1):
-            d, k = home[t]
-            out_ref[TILE * t : TILE * (t + 1), :] = returned_ref[d, TILE * k : TILE * (k + 1), :]
+        both = []
+        for d, k in (home[2 * pair], home[2 * pair + 1]):
+            both += [returned_ref[d, 2 * k + half].astype(F32) for half in range(2)]
+        out_ref[16 * pair : 16 * (pair + 1), :] = jnp.concatenate(both, axis=0).astype(BF)
     spare = []
     for tile in range(left // TILE):
-        heads = [returned_ref[TILE * tile + r].astype(F32)[kept : kept + 1] for r in range(TILE)]
+        heads = [returned_ref[TILE * tile + r, kept // QUAD].astype(F32)[:1] for r in range(TILE)]
         spare.append(stack_rows(heads))
     out_ref[devices * each :, :] = jnp.concatenate(spare, axis=0).astype(BF)
     collect(devices, section, returned_ref, wet_ref, stress_ref)
@@ -515,6 +518,7 @@
         out_specs=vmem(),
         compiler_params=params,
     )(returned, wet)
+    returned = returned.reshape(devices, -1, LAT)
     main = returned[:, :each].reshape(devices * each, LAT)
     return jnp.concatenate([main, returned[:left, kept]], axis=0), stress
 

time: 42.4 us -> 41.7 us (0.983)
  blocking collectives: 36.4 us -> 35.7 us
    all_to_all x1, blocking collectives: 15.6 us -> 14.9 us  [on_device(): lax.all_to_all(leaving, AXES, split_axis=0, concat_axis=0, tiled=True)]
where the time goes in v5:
time: 41.7 us; the launch traced here: 41.5 us
  blocking collectives  35.7 us (86%)
  Pallas kernels  4.38 us (11%)
  between operations  1.33 us (3%)
    all_to_all x1, blocking collectives, on_device(): lax.all_to_all(sending, AXES, split_axis=0, concat_axis=0, tiled=True)  20.9 us
    all_to_all x1, blocking collectives, on_device(): lax.all_to_all(leaving, AXES, split_axis=0, concat_axis=0, tiled=True)  14.9 us
    pallas_call x1, Pallas kernels, packed(): pl.pallas_call(functools.partial(pack_kernel, devices, section), out_shap...  1.92 us
    pallas_call x1, Pallas kernels, spread(): pl.pallas_call(functools.partial(spread_kernel, devices, section), out_sh...  1.62 us
    pallas_call x1, Pallas kernels, unpacked(): pl.pallas_call(functools.partial(unpack_kernel, devices, section), out_sh...  0.84 us

profile of v5, /device:TPU:0, one launch (start us, length us, event | category | flops | bytes accessed | tf_op | source)
XLA Modules:
  0.0 41.5 jit_solution(18118879257840097653)
XLA Ops:
  1.3 1.9 %shard_map.77 = (bf16[32,48,128]{2,1,0:T(8,128)(2,1)}, f32[48,128]{1,0:T(8,128)}) custom-call(s32[1]{0:T(128)S(6)} %copy.8.order_ref, bf16[1296,128]{1,0:T(8,128)(2,1)} %spectrum_ref.1, f32[2,128]{1,0:T(2,128)} %wind_hbm.1, f32[1,128]{1,0:T(1,128)} %bitcast.1, f32[32,48,128]{2,1,0:T(8,128)} %constant.4.clone.tables_hbm), custom_call_target="tpu_custom_call" | custom-call | tf_op jit(solution)/shard_map/pallas_call | solution.py:277
  3.2 0.0 copy-start
  3.2 0.0 copy-start.1
  3.2 0.0 copy-start.2
  3.2 20.9 %all_to_all.10.recv_ref = bf16[32,48,128]{2,1,0:T(8,128)(2,1)S(1)} all-to-all(bf16[32,48,128]{2,1,0:T(8,128)(2,1)} %get-tuple-element.4), channel_id=1, replica_groups=mesh['sec'=4,'dom'=8] {'sec','dom'}, dimensions={0} | all-to-all | bytes 786432 | tf_op jit(solution)/shard_map/all_to_all | solution.py:529
  24.1 0.0 copy-done
  24.1 0.0 copy-done.1
  24.1 0.0 copy-done.2
  24.1 1.6 %shard_map.78 = bf16[32,11,4,128]{3,2,1,0:T(4,128)(2,1)S(1)} custom-call(s32[1]{0:T(128)S(6)} %copy.8.order_ref, bf16[32,48,128]{2,1,0:T(8,128)(2,1)S(1)} %all_to_all.10.recv_ref, bf16[1296,128]{1,0:T(8,128)(2,1)S(1)} %copy-done, f32[48,128]{1,0:T(8,128)S(1)} %copy-done.2, f32[72,128]{1,0:T(8,128)S(1)} %copy-done.1), custom_call_target="tpu_custom_call" | custom-call | tf_op jit(solution)/shard_map/pallas_call | solution.py:454
  25.7 0.0 copy-start.3
  25.8 14.9 %all_to_all.11.returned_ref = bf16[32,11,4,128]{3,2,1,0:T(4,128)(2,1)S(1)} all-to-all(bf16[32,11,4,128]{3,2,1,0:T(4,128)(2,1)S(1)} %shard_map.78), channel_id=1, replica_groups=mesh['sec'=4,'dom'=8] {'sec','dom'}, dimensions={0} | all-to-all | bytes 720896 | tf_op jit(solution)/shard_map/all_to_all | solution.py:531
  40.6 0.0 copy-done.3
  40.6 0.8 %shard_map.79 = (bf16[1296,128]{1,0:T(8,128)(2,1)}, f32[2,128]{1,0:T(2,128)}) custom-call(bf16[32,11,4,128]{3,2,1,0:T(4,128)(2,1)S(1)} %all_to_all.11.returned_ref, f32[1,128]{1,0:T(1,128)S(1)} %bitcast.2), custom_call_target="tpu_custom_call" | custom-call | tf_op jit(solution)/shard_map/pallas_call | solution.py:507
Async XLA Ops:
  3.2 20.9 %copy-start = (bf16[1296,128]{1,0:T(8,128)(2,1)S(1)}, bf16[1296,128]{1,0:T(8,128)(2,1)}, u32[]{:S(2)}) copy-start(bf16[1296,128]{1,0:T(8,128)(2,1)} %spectrum_ref.1) | copy-start | bytes 995332
  3.2 20.9 %copy-start.1 = (f32[72,128]{1,0:T(8,128)S(1)}, f32[72,128]{1,0:T(8,128)}, u32[]{:S(2)}) copy-start(f32[72,128]{1,0:T(8,128)} %constant.5.clone.angle_ref) | copy-start | bytes 110596
  3.2 20.9 %copy-start.2 = (f32[48,128]{1,0:T(8,128)S(1)}, f32[48,128]{1,0:T(8,128)}, u32[]{:S(2)}) copy-start(f32[48,128]{1,0:T(8,128)} %get-tuple-element.5.table_ref) | copy-start | bytes 73732
  25.7 14.9 %copy-start.3 = (f32[128]{0:T(128)S(1)}, f32[128]{0:T(128)}, u32[]{:S(2)}) copy-start(f32[128]{0:T(128)} %param.8) | copy-start | bytes 1540

commit v6 on v5

--- a/solution.py
+++ b/solution.py
@@ -270,9 +270,10 @@
             pltpu.VMEM((1, LAT), F32),
             pltpu.SemaphoreType.DMA((PARTS + 3,)),
         ],
-        compiler_params=pltpu.CompilerParams(vmem_limit_bytes=60 << 20),
+        compiler_params=pltpu.CompilerParams(vmem_limit_bytes=24 << 20),
     )
-    operands = (block_order, spectrum, surface_wind, wet, jnp.asarray(device_tables(devices)))
+    stay = (spectrum, surface_wind, wet, jnp.asarray(device_tables(devices)))
+    operands = (block_order, *(pltpu.with_memory_space_constraint(array, pltpu.HBM) for array in stay))
     if each == kept:
         return pl.pallas_call(
             functools.partial(pack_kernel, devices, section),

time: 41.7 us -> 40.7 us (0.976)
  Pallas kernels: 4.38 us -> 3.63 us
    pallas_call x1, Pallas kernels: 1.92 us -> 1.17 us  [packed(): pl.pallas_call(functools.partial(pack_kernel, devices, section), out_shap...]
where the time goes in v6:
time: 40.7 us; the launch traced here: 40.5 us
  blocking collectives  35.5 us (87%)
  Pallas kernels  3.63 us (9%)
  between operations  1.32 us (3%)
    all_to_all x1, blocking collectives, on_device(): lax.all_to_all(sending, AXES, split_axis=0, concat_axis=0, tiled=True)  20.6 us
    all_to_all x1, blocking collectives, on_device(): lax.all_to_all(leaving, AXES, split_axis=0, concat_axis=0, tiled=True)  14.9 us
    pallas_call x1, Pallas kernels, spread(): pl.pallas_call(functools.partial(spread_kernel, devices, section), out_sh...  1.62 us
    pallas_call x1, Pallas kernels, packed(): pl.pallas_call(functools.partial(pack_kernel, devices, section), out_shap...  1.17 us
    pallas_call x1, Pallas kernels, unpacked(): pl.pallas_call(functools.partial(unpack_kernel, devices, section), out_sh...  0.84 us

profile of v6, /device:TPU:0, one launch (start us, length us, event | category | flops | bytes accessed | tf_op | source)
XLA Modules:
  0.0 40.5 jit_solution(14149448125615235475)
XLA Ops:
  1.3 1.2 %shard_map.77 = (bf16[32,48,128]{2,1,0:T(8,128)(2,1)S(1)}, f32[48,128]{1,0:T(8,128)S(1)}) custom-call(s32[1]{0:T(128)S(6)} %copy.8.order_ref, bf16[1296,128]{1,0:T(8,128)(2,1)} %spectrum_ref.1, f32[2,128]{1,0:T(2,128)} %wind_hbm.1, f32[1,128]{1,0:T(1,128)} %bitcast.1, f32[32,48,128]{2,1,0:T(8,128)} %constant.4.clone.tables_hbm), custom_call_target="tpu_custom_call" | custom-call | tf_op jit(solution)/shard_map/pallas_call | solution.py:278
  2.5 0.0 copy-start
  2.5 0.0 copy-start.1
  2.5 20.6 %all_to_all.10.recv_ref = bf16[32,48,128]{2,1,0:T(8,128)(2,1)S(1)} all-to-all(bf16[32,48,128]{2,1,0:T(8,128)(2,1)S(1)} %get-tuple-element.4), channel_id=1, replica_groups=mesh['sec'=4,'dom'=8] {'sec','dom'}, dimensions={0} | all-to-all | bytes 786432 | tf_op jit(solution)/shard_map/all_to_all | solution.py:530
  23.1 0.0 copy-done
  23.1 0.0 copy-done.1
  23.1 1.6 %shard_map.78 = bf16[32,11,4,128]{3,2,1,0:T(4,128)(2,1)S(1)} custom-call(s32[1]{0:T(128)S(6)} %copy.8.order_ref, bf16[32,48,128]{2,1,0:T(8,128)(2,1)S(1)} %all_to_all.10.recv_ref, bf16[1296,128]{1,0:T(8,128)(2,1)S(1)} %copy-done, f32[48,128]{1,0:T(8,128)S(1)} %get-tuple-element.5.table_ref, f32[72,128]{1,0:T(8,128)S(1)} %copy-done.1), custom_call_target="tpu_custom_call" | custom-call | tf_op jit(solution)/shard_map/pallas_call | solution.py:455
  24.8 0.0 copy-start.2
  24.8 14.9 %all_to_all.11.returned_ref = bf16[32,11,4,128]{3,2,1,0:T(4,128)(2,1)S(1)} all-to-all(bf16[32,11,4,128]{3,2,1,0:T(4,128)(2,1)S(1)} %shard_map.78), channel_id=1, replica_groups=mesh['sec'=4,'dom'=8] {'sec','dom'}, dimensions={0} | all-to-all | bytes 720896 | tf_op jit(solution)/shard_map/all_to_all | solution.py:532
  39.6 0.0 copy-done.2
  39.7 0.8 %shard_map.79 = (bf16[1296,128]{1,0:T(8,128)(2,1)}, f32[2,128]{1,0:T(2,128)}) custom-call(bf16[32,11,4,128]{3,2,1,0:T(4,128)(2,1)S(1)} %all_to_all.11.returned_ref, f32[1,128]{1,0:T(1,128)S(1)} %bitcast.2), custom_call_target="tpu_custom_call" | custom-call | tf_op jit(solution)/shard_map/pallas_call | solution.py:508
Async XLA Ops:
  2.5 20.7 %copy-start = (bf16[1296,128]{1,0:T(8,128)(2,1)S(1)}, bf16[1296,128]{1,0:T(8,128)(2,1)}, u32[]{:S(2)}) copy-start(bf16[1296,128]{1,0:T(8,128)(2,1)} %spectrum_ref.1) | copy-start | bytes 995332
  2.5 20.7 %copy-start.1 = (f32[72,128]{1,0:T(8,128)S(1)}, f32[72,128]{1,0:T(8,128)}, u32[]{:S(2)}) copy-start(f32[72,128]{1,0:T(8,128)} %constant.5.clone.angle_ref) | copy-start | bytes 110596
  24.8 14.9 %copy-start.2 = (f32[128]{0:T(128)S(1)}, f32[128]{0:T(128)}, u32[]{:S(2)}) copy-start(f32[128]{0:T(128)} %param.8) | copy-start | bytes 1540

commit v7 on v6

--- a/solution.py
+++ b/solution.py
@@ -71,14 +71,29 @@
     for t in range(devices * count):
         wave = SIN[(TILE * t + np.arange(TILE)) % ND]
         ways[0 if (wave >= 0).all() else 1 if (wave <= 0).all() else 2].append(t)
+    def eastward(t):
+        return (COS[(TILE * t + np.arange(TILE)) % ND] >= 0).all()
+
+    def westward(t):
+        return (COS[(TILE * t + np.arange(TILE)) % ND] <= 0).all()
+
+    ways[0].sort(key=lambda t: (not eastward(t), t))
+    ways[1].sort(key=lambda t: (not eastward(t), t))
     sure = min(len(ways[0]) // half, len(ways[1]) // half, count)
-    rest = sorted(ways[0][sure * half :] + ways[1][sure * half :] + ways[2])
+    rest = sorted(ways[0][sure * half :] + ways[1][sure * half :] + ways[2], key=lambda t: (not westward(t), t))
     slots = []
     for d in range(devices):
         way, place = ways[d // half], d % half
-        mixed = rest[(count - sure) * d : (count - sure) * (d + 1)]
-        slots.append(way[sure * place : sure * (place + 1)] + mixed)
+        slots.append([way[half * k + place] for k in range(sure)] + [rest[devices * k + d] for k in range(count - sure)])
     return slots, sure
+
+
+def column_way(devices, k):
+    slots = tile_slots(devices)[0]
+    if slots is None or k >= len(slots[0]):
+        return 0
+    wave = np.concatenate([COS[(TILE * tiles[k] + np.arange(TILE)) % ND] for tiles in slots])
+    return 1 if (wave >= 0).all() else -1 if (wave <= 0).all() else 0
 
 
 def spare_way(devices):
@@ -403,6 +418,7 @@
         westerly, southerly = from_west > 0.0, from_south > 0.0
         from_x, from_y = from_west + from_east, from_south + from_north
         way = spare_way(devices) if TILE * t == kept else 0
+        aside = column_way(devices, t)
 
         def shifted(here):
             if t < sure:
@@ -414,7 +430,11 @@
         def moved(column):
             west, east = around(column)
             here = source[column, part, :]
-            total = keep * here + from_x * jnp.where(westerly, source[west, part, :], source[east, part, :])
+            if aside:
+                beside = source[west if aside > 0 else east, part, :]
+            else:
+                beside = jnp.where(westerly, source[west, part, :], source[east, part, :])
+            total = keep * here + from_x * beside
             return wet_ref[column] * (total + from_y * shifted(here))
 
         return moved

time: 40.7 us -> 40.7 us (level)
  no operation moved by 1% of the time
where the time goes in v7:
time: 40.7 us; the launch traced here: 40.5 us
  blocking collectives  35.5 us (87%)
  Pallas kernels  3.61 us (9%)
  between operations  1.32 us (3%)
    all_to_all x1, blocking collectives, on_device(): lax.all_to_all(sending, AXES, split_axis=0, concat_axis=0, tiled=True)  20.6 us
    all_to_all x1, blocking collectives, on_device(): lax.all_to_all(leaving, AXES, split_axis=0, concat_axis=0, tiled=True)  14.9 us
    pallas_call x1, Pallas kernels, spread(): pl.pallas_call(functools.partial(spread_kernel, devices, section), out_sh...  1.6 us
    pallas_call x1, Pallas kernels, packed(): pl.pallas_call(functools.partial(pack_kernel, devices, section), out_shap...  1.17 us
    pallas_call x1, Pallas kernels, unpacked(): pl.pallas_call(functools.partial(unpack_kernel, devices, section), out_sh...  0.84 us

profile of v7, /device:TPU:0, one launch (start us, length us, event | category | flops | bytes accessed | tf_op | source)
XLA Modules:
  0.0 40.5 jit_solution(11061365878636681828)
XLA Ops:
  1.3 1.2 %shard_map.77 = (bf16[32,48,128]{2,1,0:T(8,128)(2,1)S(1)}, f32[48,128]{1,0:T(8,128)S(1)}) custom-call(s32[1]{0:T(128)S(6)} %copy.8.order_ref, bf16[1296,128]{1,0:T(8,128)(2,1)} %spectrum_ref.1, f32[2,128]{1,0:T(2,128)} %wind_hbm.1, f32[1,128]{1,0:T(1,128)} %bitcast.1, f32[32,48,128]{2,1,0:T(8,128)} %constant.4.clone.tables_hbm), custom_call_target="tpu_custom_call" | custom-call | tf_op jit(solution)/shard_map/pallas_call | solution.py:293
  2.5 0.0 copy-start
  2.5 0.0 copy-start.1
  2.5 20.6 %all_to_all.10.recv_ref = bf16[32,48,128]{2,1,0:T(8,128)(2,1)S(1)} all-to-all(bf16[32,48,128]{2,1,0:T(8,128)(2,1)S(1)} %get-tuple-element.4), channel_id=1, replica_groups=mesh['sec'=4,'dom'=8] {'sec','dom'}, dimensions={0} | all-to-all | bytes 786432 | tf_op jit(solution)/shard_map/all_to_all | solution.py:550
  23.1 0.0 copy-done
  23.1 0.0 copy-done.1
  23.1 1.6 %shard_map.78 = bf16[32,11,4,128]{3,2,1,0:T(4,128)(2,1)S(1)} custom-call(s32[1]{0:T(128)S(6)} %copy.8.order_ref, bf16[32,48,128]{2,1,0:T(8,128)(2,1)S(1)} %all_to_all.10.recv_ref, bf16[1296,128]{1,0:T(8,128)(2,1)S(1)} %copy-done, f32[48,128]{1,0:T(8,128)S(1)} %get-tuple-element.5.table_ref, f32[72,128]{1,0:T(8,128)S(1)} %copy-done.1), custom_call_target="tpu_custom_call" | custom-call | tf_op jit(solution)/shard_map/pallas_call | solution.py:475
  24.7 0.0 copy-start.2
  24.8 14.9 %all_to_all.11.returned_ref = bf16[32,11,4,128]{3,2,1,0:T(4,128)(2,1)S(1)} all-to-all(bf16[32,11,4,128]{3,2,1,0:T(4,128)(2,1)S(1)} %shard_map.78), channel_id=1, replica_groups=mesh['sec'=4,'dom'=8] {'sec','dom'}, dimensions={0} | all-to-all | bytes 720896 | tf_op jit(solution)/shard_map/all_to_all | solution.py:552
  39.6 0.0 copy-done.2
  39.6 0.8 %shard_map.79 = (bf16[1296,128]{1,0:T(8,128)(2,1)}, f32[2,128]{1,0:T(2,128)}) custom-call(bf16[32,11,4,128]{3,2,1,0:T(4,128)(2,1)S(1)} %all_to_all.11.returned_ref, f32[1,128]{1,0:T(1,128)S(1)} %bitcast.2), custom_call_target="tpu_custom_call" | custom-call | tf_op jit(solution)/shard_map/pallas_call | solution.py:528
Async XLA Ops:
  2.5 20.7 %copy-start = (bf16[1296,128]{1,0:T(8,128)(2,1)S(1)}, bf16[1296,128]{1,0:T(8,128)(2,1)}, u32[]{:S(2)}) copy-start(bf16[1296,128]{1,0:T(8,128)(2,1)} %spectrum_ref.1) | copy-start | bytes 995332
  2.5 20.7 %copy-start.1 = (f32[72,128]{1,0:T(8,128)S(1)}, f32[72,128]{1,0:T(8,128)}, u32[]{:S(2)}) copy-start(f32[72,128]{1,0:T(8,128)} %constant.5.clone.angle_ref) | copy-start | bytes 110596
  24.7 14.9 %copy-start.2 = (f32[128]{0:T(128)S(1)}, f32[128]{0:T(128)}, u32[]{:S(2)}) copy-start(f32[128]{0:T(128)} %param.8) | copy-start | bytes 1540

commit v8 on v7

--- a/solution.py
+++ b/solution.py
@@ -427,13 +427,22 @@
                 return pltpu.roll(here, way % LAT, 1)
             return jnp.where(southerly, pltpu.roll(here, 1, 1), pltpu.roll(here, LAT - 1, 1))
 
+        held = {}
+
+        def load(column):
+            if not isinstance(column, int):
+                return source[column, part, :]
+            if column not in held:
+                held[column] = source[column, part, :]
+            return held[column]
+
         def moved(column):
             west, east = around(column)
-            here = source[column, part, :]
+            here = load(column)
             if aside:
-                beside = source[west if aside > 0 else east, part, :]
+                beside = load(west if aside > 0 else east)
             else:
-                beside = jnp.where(westerly, source[west, part, :], source[east, part, :])
+                beside = jnp.where(westerly, load(west), load(east))
             total = keep * here + from_x * beside
             return wet_ref[column] * (total + from_y * shifted(here))
 

time: 40.7 us -> 40.7 us (level)
  no operation moved by 1% of the time
where the time goes in v8:
time: 40.7 us; the launch traced here: 40.5 us
  blocking collectives  35.5 us (87%)
  Pallas kernels  3.61 us (9%)
  between operations  1.32 us (3%)
    all_to_all x1, blocking collectives, on_device(): lax.all_to_all(sending, AXES, split_axis=0, concat_axis=0, tiled=True)  20.6 us
    all_to_all x1, blocking collectives, on_device(): lax.all_to_all(leaving, AXES, split_axis=0, concat_axis=0, tiled=True)  14.9 us
    pallas_call x1, Pallas kernels, spread(): pl.pallas_call(functools.partial(spread_kernel, devices, section), out_sh...  1.6 us
    pallas_call x1, Pallas kernels, packed(): pl.pallas_call(functools.partial(pack_kernel, devices, section), out_shap...  1.17 us
    pallas_call x1, Pallas kernels, unpacked(): pl.pallas_call(functools.partial(unpack_kernel, devices, section), out_sh...  0.84 us

profile of v8, /device:TPU:0, one launch (start us, length us, event | category | flops | bytes accessed | tf_op | source)
XLA Modules:
  0.0 40.5 jit_solution(11061365878636681828)
XLA Ops:
  1.3 1.2 %shard_map.77 = (bf16[32,48,128]{2,1,0:T(8,128)(2,1)S(1)}, f32[48,128]{1,0:T(8,128)S(1)}) custom-call(s32[1]{0:T(128)S(6)} %copy.8.order_ref, bf16[1296,128]{1,0:T(8,128)(2,1)} %spectrum_ref.1, f32[2,128]{1,0:T(2,128)} %wind_hbm.1, f32[1,128]{1,0:T(1,128)} %bitcast.1, f32[32,48,128]{2,1,0:T(8,128)} %constant.4.clone.tables_hbm), custom_call_target="tpu_custom_call" | custom-call | tf_op jit(solution)/shard_map/pallas_call | solution.py:293
  2.5 0.0 copy-start
  2.5 0.0 copy-start.1
  2.5 20.6 %all_to_all.10.recv_ref = bf16[32,48,128]{2,1,0:T(8,128)(2,1)S(1)} all-to-all(bf16[32,48,128]{2,1,0:T(8,128)(2,1)S(1)} %get-tuple-element.4), channel_id=1, replica_groups=mesh['sec'=4,'dom'=8] {'sec','dom'}, dimensions={0} | all-to-all | bytes 786432 | tf_op jit(solution)/shard_map/all_to_all | solution.py:559
  23.1 0.0 copy-done
  23.1 0.0 copy-done.1
  23.1 1.6 %shard_map.78 = bf16[32,11,4,128]{3,2,1,0:T(4,128)(2,1)S(1)} custom-call(s32[1]{0:T(128)S(6)} %copy.8.order_ref, bf16[32,48,128]{2,1,0:T(8,128)(2,1)S(1)} %all_to_all.10.recv_ref, bf16[1296,128]{1,0:T(8,128)(2,1)S(1)} %copy-done, f32[48,128]{1,0:T(8,128)S(1)} %get-tuple-element.5.table_ref, f32[72,128]{1,0:T(8,128)S(1)} %copy-done.1), custom_call_target="tpu_custom_call" | custom-call | tf_op jit(solution)/shard_map/pallas_call | solution.py:484
  24.7 0.0 copy-start.2
  24.8 14.9 %all_to_all.11.returned_ref = bf16[32,11,4,128]{3,2,1,0:T(4,128)(2,1)S(1)} all-to-all(bf16[32,11,4,128]{3,2,1,0:T(4,128)(2,1)S(1)} %shard_map.78), channel_id=1, replica_groups=mesh['sec'=4,'dom'=8] {'sec','dom'}, dimensions={0} | all-to-all | bytes 720896 | tf_op jit(solution)/shard_map/all_to_all | solution.py:561
  39.6 0.0 copy-done.2
  39.6 0.8 %shard_map.79 = (bf16[1296,128]{1,0:T(8,128)(2,1)}, f32[2,128]{1,0:T(2,128)}) custom-call(bf16[32,11,4,128]{3,2,1,0:T(4,128)(2,1)S(1)} %all_to_all.11.returned_ref, f32[1,128]{1,0:T(1,128)S(1)} %bitcast.2), custom_call_target="tpu_custom_call" | custom-call | tf_op jit(solution)/shard_map/pallas_call | solution.py:537
Async XLA Ops:
  2.5 20.7 %copy-start = (bf16[1296,128]{1,0:T(8,128)(2,1)S(1)}, bf16[1296,128]{1,0:T(8,128)(2,1)}, u32[]{:S(2)}) copy-start(bf16[1296,128]{1,0:T(8,128)(2,1)} %spectrum_ref.1) | copy-start | bytes 995332
  2.5 20.7 %copy-start.1 = (f32[72,128]{1,0:T(8,128)S(1)}, f32[72,128]{1,0:T(8,128)}, u32[]{:S(2)}) copy-start(f32[72,128]{1,0:T(8,128)} %constant.5.clone.angle_ref) | copy-start | bytes 110596
  24.7 14.9 %copy-start.2 = (f32[128]{0:T(128)S(1)}, f32[128]{0:T(128)}, u32[]{:S(2)}) copy-start(f32[128]{0:T(128)} %param.8) | copy-start | bytes 1540
